TPU v7x, 128 devices: a whole 4x4x4 slice. The times are simulated.
128 devices in a mesh: dp: 8 (over z, y_lo), fsdp: 16 (over y_hi, x, core).
Axes of the slice: x: 4, y: 4 (y_hi: 2, y_lo: 2; y = y_hi * 2 + y_lo), z: 4, core: 2. Of those that a mesh axis runs over, the one named last changes fastest.
Arguments:
- tokens: bfloat16 [4096, 3072], P('fsdp'), may hold values from -6 to 6
- cotangent: bfloat16 [4096, 3072], P('fsdp'), may hold values from -6 to 6
- w_in: bfloat16 [3072, 12288], P('fsdp', 'dp'), may hold values from -0.4690971 to 0.4690971
- w_out: bfloat16 [12288, 3072], P('dp', 'fsdp'), may hold values from -0.23454855 to 0.23454855
Outputs:
- grad_in: float32 [3072, 12288], P('fsdp', 'dp')
- grad_out: float32 [12288, 3072], P('dp', 'fsdp')
- input_grad: bfloat16 [4096, 3072], P('fsdp')
All inputs are finite; a program needn't handle non-finite values.
Results may differ from a plain program's by a relative error of at most 0.019.
Values may be sent and summed in bfloat16 or wider, within the bound.
A program may use at most 192 MiB of HBM per device.

v0:
```python
import math

import jax
import jax.numpy as jnp
from jax import lax
from jax.sharding import PartitionSpec as P

D = 3072
FF = 12288


RADIUS_SHARE = 0.5
EPSILON = 1e-06


def gelu_exact(values):
    return jax.nn.gelu(values, approximate=False)


def contract_rows(first_op, second_op):
    return lax.dot_general(
        first_op, second_op, (((0,), (0,)), ((), ())), preferred_element_type=jnp.float32
    )


def contract_cols(first_op, second_op):
    return lax.dot_general(
        first_op, second_op, (((1,), (1,)), ((), ())), preferred_element_type=jnp.float32
    )


def on_device(tokens, cotangent, w_in, w_out):
    radius = RADIUS_SHARE * math.sqrt(D + FF)
    grad_scale = 1.0 / math.sqrt(tokens.shape[0] * lax.axis_size("fsdp"))
    out_width = w_in.shape[1]
    full_in, full_out = (
        lax.all_gather(w_in, "fsdp", axis=0, tiled=True),
        lax.all_gather(w_out, "fsdp", axis=1, tiled=True),
    )
    hidden_one = jnp.dot(tokens, full_in, preferred_element_type=jnp.float32)
    back_one = contract_cols(cotangent, full_out)
    active_one, pullback_one = jax.vjp(gelu_exact, hidden_one)
    slope_one = pullback_one(back_one)[0].astype(jnp.bfloat16)
    active_one = active_one.astype(jnp.bfloat16)
    ascent_in = contract_rows(tokens, slope_one)
    ascent_out = contract_rows(active_one, cotangent)
    local_square = jnp.sum(ascent_in * ascent_in) + jnp.sum(ascent_out * ascent_out)
    group_square = lax.psum(local_square, "dp")
    factor = radius / jnp.sqrt(group_square + EPSILON)
    moved_in = (full_in + factor * ascent_in).astype(jnp.bfloat16)
    moved_out = (full_out + factor * ascent_out).astype(jnp.bfloat16)
    hidden_two = jnp.dot(tokens, moved_in, preferred_element_type=jnp.float32)
    active_two, pullback_two = jax.vjp(gelu_exact, hidden_two)
    active_two = active_two.astype(jnp.bfloat16)
    back_two = contract_cols(cotangent, moved_out)
    slope_two = pullback_two(back_two)[0].astype(jnp.bfloat16)
    both_shares = lax.psum_scatter(
        jnp.concatenate(
            [contract_rows(tokens, slope_two), contract_rows(cotangent, active_two)], axis=1
        ).astype(jnp.bfloat16),
        "fsdp",
        scatter_dimension=0,
        tiled=True,
    ).astype(jnp.float32)
    in_share = both_shares[:, :out_width]
    out_share = both_shares[:, out_width:]
    partial_input = contract_cols(slope_two, moved_in)
    input_grad = lax.psum(partial_input.astype(jnp.bfloat16), "dp")
    return (in_share * grad_scale, jnp.transpose(out_share * grad_scale), input_grad)


def solution(mesh):
    return jax.shard_map(
        on_device,
        mesh=mesh,
        in_specs=(P("fsdp", None), P("fsdp", None), P("fsdp", "dp"), P("dp", "fsdp")),
        out_specs=(P("fsdp", "dp"), P("dp", "fsdp"), P("fsdp", None)),
        check_vma=False,
    )
```

profile of v0, /device:TPU:0, one launch (start us, length us, event | category | flops | bytes accessed | tf_op | source)
XLA Modules:
  0.0 578.8 jit_solution(17734586128913702336)
XLA Ops:
  8.7 81.3 %all-gather.3.cloned.1.call-done = bf16[3072,1536]{1,0:T(8,128)(2,1)} async-done(((bf16[192,1536]{1,0:T(8,128)(2,1)}), bf16[3072,1536]{1,0:T(8,128)(2,1)}) %all-gather.3.cloned.1.call-update) | async-done | bytes 9437200 | tf_op jit(solution)/shard_map/all_gather | solution.py:37
  90.0 5.6 fusion.50
  96.8 11.5 %multiply_reduce_fusion = (f32[]{:T(128)}, f32[1536,3072]{1,0:T(8,128)}) fusion(bf16[256,3072]{1,0:T(8,128)(2,1)S(1)} %copy-done, f32[256,1536]{1,0:T(8,128)S(1)} %fusion.50), kind=kOutput, calls=%fused_computation.4 | convolution fusion | flops 2450915328 | bytes 22020100 | tf_op jit(solution)/shard_map/dot_general | solution.py:21
  108.3 59.1 %all-gather.5.cloned.1.call-done = bf16[1536,3072]{0,1:T(8,128)(2,1)} async-done(((bf16[1536,192]{0,1:T(8,128)(2,1)}), bf16[1536,3072]{0,1:T(8,128)(2,1)}) %all-gather.5.cloned.1.call-update) | async-done | bytes 9437200 | tf_op jit(solution)/shard_map/all_gather | solution.py:38
  167.4 5.3 fusion.51
  172.7 11.9 %multiply_reduce_fusion.1 = (f32[]{:T(128)}, f32[1536,3072]{1,0:T(8,128)}) fusion(bf16[256,3072]{1,0:T(8,128)(2,1)S(1)} %copy-done.3, f32[256,1536]{1,0:T(8,128)S(1)} %fusion.51, f32[256,1536]{1,0:T(8,128)S(1)} %copy-done.7), kind=kOutput, calls=%fused_computation.5 | convolution fusion | flops 2453667840 | bytes 23592964 | tf_op jit(solution)/shard_map/dot_general | solution.py:21
  185.9 19.7 %psum.14 = f32[]{:T(128)} all-reduce(f32[]{:T(128)S(6)} %add.18), channel_id=1, replica_groups=mesh['dp'=8,'fsdp'=16] {'dp'}, use_global_device_ids=true, to_apply=%region_2.0 | all-reduce | flops 1 | bytes 8 | tf_op jit(solution)/shard_map/psum | solution.py:48
  206.3 12.6 %copy.14 = bf16[3072,1536]{0,1:T(8,128)(2,1)} copy(bf16[3072,1536]{1,0:T(8,128)(2,1)} %all-gather.3.cloned.1.call-done) | data formatting | bytes 18874368 | tf_op jit(solution)/shard_map/all_gather | solution.py:37
  218.9 10.1 %fusion = bf16[3072,1536]{0,1:T(8,128)(2,1)S(1)} fusion(f32[1536,3072]{1,0:T(8,128)} %get-tuple-element.12, bf16[3072,1536]{0,1:T(8,128)(2,1)} %copy.14, f32[]{:T(128)S(6)} %div.3), kind=kLoop, calls=%fused_computation.2 | loop fusion | flops 18874368 | bytes 37748740 | tf_op jit(solution)/shard_map/convert_element_type | solution.py:50
  229.1 3.6 copy-done.2
  232.7 2.8 fusion.52
  236.7 8.3 %fusion.2 = bf16[3072,1536]{0,1:T(8,128)(2,1)} fusion(bf16[256,3072]{1,0:T(8,128)(2,1)S(1)} %copy-done, f32[1536,256]{0,1:T(8,128)S(1)} %fusion.52), kind=kOutput, calls=%fused_computation.9 | convolution fusion | flops 2446196736 | bytes 12582912 | tf_op jit(solution)/shard_map/dot_general | solution.py:21
  245.0 12.8 %copy.16 = bf16[1536,3072]{1,0:T(8,128)(2,1)} copy(bf16[1536,3072]{0,1:T(8,128)(2,1)} %all-gather.5.cloned.1.call-done) | data formatting | bytes 18874368 | tf_op jit(solution)/shard_map/all_gather | solution.py:38
  257.7 12.9 %fusion.15 = bf16[256,1536]{1,0:T(8,128)(2,1)S(1)} fusion(bf16[256,3072]{1,0:T(8,128)(2,1)S(1)} %copy-done, f32[1536,3072]{1,0:T(8,128)} %get-tuple-element.14, bf16[1536,3072]{1,0:T(8,128)(2,1)} %copy.16, f32[]{:T(128)S(6)} %div.3, f32[1536,256]{0,1:T(8,128)} %copy-done.5), kind=kOutput, calls=%fused_computation.33 | convolution fusion | flops 2463105024 | bytes 32243716 | tf_op jit(solution)/shard_map/dot_general | solution.py:27
  270.6 2.9 fusion.1
  273.6 26.8 %pad_maximum_fusion = bf16[3072,3072]{0,1:T(8,128)(2,1)} fusion(bf16[3072,1536]{0,1:T(8,128)(2,1)S(1)} %bitcast.108, bf16[3072,1536]{0,1:T(8,128)(2,1)S(1)} %fusion.1), kind=kLoop, calls=%fused_computation | loop fusion | flops 37748736 | bytes 37748736 | tf_op jit(solution)/shard_map/concatenate | solution.py:58
  300.4 24.6 %copy.23 = bf16[3072,3072]{1,0:T(8,128)(2,1)} copy(bf16[3072,3072]{0,1:T(8,128)(2,1)} %pad_maximum_fusion) | data formatting | bytes 37748736
  325.1 7.4 %convolution_convert_fusion.2 = bf16[256,3072]{1,0:T(8,128)(2,1)} fusion(bf16[256,1536]{1,0:T(8,128)(2,1)S(1)} %fusion.15, bf16[3072,1536]{0,1:T(8,128)(2,1)} %copy-done.2), kind=kOutput, calls=%fused_computation.12 | convolution fusion | flops 2416705536 | bytes 11796480 | tf_op jit(solution)/shard_map/dot_general | solution.py:27
  332.5 148.4 %reduce-scatter.4.cloned.1.call-done = bf16[192,3072]{1,0:T(8,128)(2,1)} async-done(((bf16[3072,3072]{1,0:T(8,128)(2,1)}), bf16[192,3072]{1,0:T(8,128)(2,1)}) %reduce-scatter.4.cloned.1.call-update) | async-done | bytes 1179664
  480.9 1.6 copy.24
  483.0 1.5 copy.20
  484.5 1.5 copy.19
  485.9 83.7 %all-reduce.2.cloned.1.call-done = bf16[256,3072]{1,0:T(8,128)(2,1)} async-done(((bf16[256,3072]{1,0:T(8,128)(2,1)}), bf16[256,3072]{1,0:T(8,128)(2,1)}) %all-reduce.2.cloned.1.call-update) | async-done | bytes 1572880 | tf_op jit(solution)/shard_map/psum | solution.py:68
  569.6 2.7 copy.26
  (32 shorter events, 4.3 us)
Async XLA Ops:
  7.2 89.6 %copy-start = (bf16[256,3072]{1,0:T(8,128)(2,1)S(1)}, bf16[256,3072]{1,0:T(8,128)(2,1)}, u32[]{:S(2)}) copy-start(bf16[256,3072]{1,0:T(8,128)(2,1)} %param.5) | copy-start | bytes 4718596
  7.2 82.8 %all-gather.3.cloned.1.call-start = ((), (), s32[]{:S(2)}) async-start(), calls=%async_computation.1 | async-start | bytes 10027008 | tf_op jit(solution)/shard_map/all_gather | solution.py:37
  7.9 159.5 %all-gather.5.cloned.1.call-start = ((), (), s32[]{:S(2)}) async-start(), calls=%async_computation.2 | async-start | bytes 10027008 | tf_op jit(solution)/shard_map/all_gather | solution.py:38
  8.7 472.2 %reduce-scatter.4.cloned.1.call-start = ((), (), s32[]{:S(2)}) async-start(), calls=%async_computation.4 | async-start | bytes 20054016
  95.7 1.1 copy-start.6
  108.3 64.3 %copy-start.3 = (bf16[256,3072]{1,0:T(8,128)(2,1)S(1)}, bf16[256,3072]{1,0:T(8,128)(2,1)}, u32[]{:S(2)}) copy-start(bf16[256,3072]{1,0:T(8,128)(2,1)} %param.4) | copy-start | bytes 4718596
  167.4 5.3 copy-start.7
  229.0 3.6 copy-start.2
  235.5 1.1 copy-start.5
  245.0 28.6 %slice-start = ((s8[9437184]{0:T(1024)(128)(4,1)}), s8[1048576]{0:T(1024)(128)(4,1)S(1)}, s32[]{:S(2)}) async-start(s8[9437184]{0:T(1024)(128)(4,1)} %bitcast.107), calls=%async_computation.5 | async-start | bytes 2097152
  257.7 12.9 %copy-start.4 = (bf16[256,3072]{1,0:T(8,128)(2,1)S(1)}, bf16[256,3072]{1,0:T(8,128)(2,1)}, u32[]{:S(2)}) copy-start(bf16[256,3072]{1,0:T(8,128)(2,1)} %param.4) | copy-start | bytes 4718596
  257.7 15.8 %slice-start.1 = ((s8[9437184]{0:T(1024)(128)(4,1)}), s8[4194304]{0:T(1024)(128)(4,1)S(1)}, s32[]{:S(2)}) async-start(s8[9437184]{0:T(1024)(128)(4,1)} %bitcast.107), calls=%async_computation.6 | async-start | bytes 8388608
  257.7 15.8 %slice-start.2 = ((s8[9437184]{0:T(1024)(128)(4,1)}), s8[4194304]{0:T(1024)(128)(4,1)S(1)}, s32[]{:S(2)}) async-start(s8[9437184]{0:T(1024)(128)(4,1)} %bitcast.107), calls=%async_computation.7 | async-start | bytes 8388608
  325.0 244.6 %all-reduce.2.cloned.1.call-start = ((), (), s32[]{:S(2)}) async-start(), calls=%async_computation.3 | async-start | bytes 3145728 | tf_op jit(solution)/shard_map/psum | solution.py:68
  484.5 87.8 %copy-start.1 = (bf16[256,3072]{1,0:T(8,128)(2,1)S(1)}, bf16[256,3072]{1,0:T(8,128)(2,1)}, u32[]{:S(2)}) copy-start(bf16[256,3072]{1,0:T(8,128)(2,1)} %param.5) | copy-start | bytes 4718596
Sparse Core Ops, SparseCore 0:
  10.4 79.5 all-gather.2
  92.4 74.9 all-gather.4
  325.1 155.7 reduce-scatter.3
  484.0 85.5 all-reduce.1
where the time goes:
time: 580 us; the launch traced here: 579 us
  waiting for transfers between devices  374 us (64%)
  matrix products  68.6 us (12%)
  local copies, waits for them, and re-layouts  63.2 us (11%)
  other arithmetic  37.4 us (6%)
  blocking collectives  19.7 us (3%)
  between operations  15.9 us (3%)
    unnamed x5, waiting for transfers between devices  150 us
    psum x1, waiting for transfers between devices, on_device(): input_grad = lax.psum(partial_input.astype(jnp.bfloat16), 'dp')  83.7 us
    all_gather x1, waiting for transfers between devices, on_device(): lax.all_gather(w_in, 'fsdp', axis=0, tiled=True)  81.3 us
    all_gather x1, waiting for transfers between devices, on_device(): lax.all_gather(w_out, 'fsdp', axis=1, tiled=True)  59.1 us
    unnamed x27, local copies, waits for them, and re-layouts  37.8 us
    dot_general x4, matrix products, contract_rows(): lax.dot_general(first_op, second_op, (((0,), (0,)), ((), ())), preferred_...  34.6 us
    concatenate x1, other arithmetic, on_device(): jnp.concatenate([contract_rows(tokens, slope_two), contract_rows(cotangen...  26.8 us
    dot_general x3, matrix products, contract_cols(): lax.dot_general(first_op, second_op, (((1,), (1,)), ((), ())), preferred_...  25.6 us
  transfers between devices with their start and end apart: 4, of which 4 were waited for; matrix products, arithmetic and copies ran while one was open for 5% of the time, Pallas kernels for 0%

commit v1 on v0

v1 whole, which is shorter than its diff:
```python
import math

import jax
import jax.numpy as jnp
from jax import lax
from jax.sharding import Mesh, PartitionSpec as P

D = 3072
FF = 12288
GROUP = 256

RADIUS_SHARE = 0.5
EPSILON = 1e-06
AXES = ("z", "ylo", "yhi", "x", "core")
QUAD = ("yhi", "core")
PLANE = ("z", "ylo", "yhi", "core")


def dot(a, b, dims):
    return lax.dot_general(a, b, (dims, ((), ())), preferred_element_type=jnp.float32)


def gelu_pair(h):
    cdf = 0.5 * (1.0 + lax.erf(h * (1.0 / math.sqrt(2.0))))
    pdf = jnp.exp(-0.5 * h * h) * (1.0 / math.sqrt(2.0 * math.pi))
    return h * cdf, cdf + h * pdf


def gram_apply(x, s):
    g = x.shape[0] // GROUP
    x3, s3 = x.reshape(g, GROUP, -1), s.reshape(g, GROUP, -1)
    gram = jnp.einsum("gtd,gud->gtu", x3, x3, preferred_element_type=jnp.float32)
    hi = gram.astype(jnp.bfloat16)
    lo = (gram - hi.astype(jnp.float32)).astype(jnp.bfloat16)
    mm = lambda m: jnp.einsum("gtu,guh->gth", m, s3, preferred_element_type=jnp.float32)
    return mm(hi) + mm(lo)


def on_device(tokens, cotangent, w_in, w_out):
    radius = RADIUS_SHARE * math.sqrt(D + FF)
    grad_scale = 1.0 / math.sqrt(4096)
    tok = lax.all_gather(tokens, QUAD, axis=0, tiled=True)
    cot = lax.all_gather(cotangent, QUAD, axis=0, tiled=True)
    both = jnp.stack([w_in, w_out.T])
    n = both.shape[1]
    quarter = both.shape[2] // 4
    mine = both.reshape(2, n, 4, quarter).transpose(2, 0, 1, 3)
    mine = lax.all_to_all(mine, QUAD, 0, 0)
    full = lax.all_gather(mine, "x", axis=0)
    full = full.reshape(4, 2, 2, 2, n, quarter).transpose(3, 1, 0, 2, 4, 5).reshape(2, D, quarter)
    full_in, full_out = full[0], full[1]
    hidden = dot(tok, full_in, ((1,), (0,)))
    back = dot(cot, full_out, ((1,), (0,)))
    act, der = gelu_pair(hidden)
    act1 = act.astype(jnp.bfloat16)
    slope1 = (back * der).astype(jnp.bfloat16)
    gs = gram_apply(tok, slope1)
    ga = gram_apply(cot, act1)
    g = gs.shape[0]
    square = jnp.sum(gs * slope1.reshape(gs.shape).astype(jnp.float32), axis=(1, 2)) + jnp.sum(
        ga * act1.reshape(ga.shape).astype(jnp.float32), axis=(1, 2)
    )
    square = lax.psum(square, PLANE)
    factor = (radius / jnp.sqrt(square + EPSILON))[:, None, None]
    hidden = hidden + (factor * gs).reshape(hidden.shape)
    back = back + (factor * ga).reshape(hidden.shape)
    act, der = gelu_pair(hidden)
    act2 = act.astype(jnp.bfloat16)
    slope2 = (back * der).astype(jnp.bfloat16)
    cross = jnp.einsum(
        "gth,guh->gtu", slope2.reshape(g, GROUP, -1), slope1.reshape(g, GROUP, -1), preferred_element_type=jnp.float32
    )
    cross = (factor * cross).astype(jnp.bfloat16)
    moved = jnp.einsum("gtu,gud->gtd", cross, tok.reshape(g, GROUP, D), preferred_element_type=jnp.float32)
    partial = dot(slope2, full_in, ((1,), (1,))) + moved.reshape(tok.shape)
    share = lax.psum_scatter(partial.astype(jnp.bfloat16), QUAD, scatter_dimension=0, tiled=True)
    input_grad = lax.psum(share, ("z", "ylo"))
    terms = jnp.stack([dot(tok, slope2, ((0,), (0,))), dot(cot, act2, ((0,), (0,)))]).astype(jnp.bfloat16)
    terms = terms.reshape(2, 2, 4, 2, n, quarter).transpose(2, 1, 3, 0, 4, 5)
    sums = lax.psum_scatter(terms.reshape(-1, quarter), "x", scatter_dimension=0, tiled=True)
    sums = lax.all_to_all(sums.reshape(4, 2, n, quarter), QUAD, 0, 0)
    sums = sums.transpose(1, 2, 0, 3).reshape(2, n, 4 * quarter).astype(jnp.float32) * grad_scale
    return sums[0], sums[1].T, input_grad


def solution(mesh):
    view = Mesh(mesh.devices.reshape(4, 2, 2, 4, 2), AXES)
    fsdp, dp = ("yhi", "x", "core"), ("z", "ylo")
    return jax.shard_map(
        on_device,
        mesh=view,
        in_specs=(P(fsdp, None), P(fsdp, None), P(fsdp, dp), P(dp, fsdp)),
        out_specs=(P(fsdp, dp), P(dp, fsdp), P(fsdp, None)),
        check_vma=False,
    )
```

time: 580 us -> 533 us (0.919)
  blocking collectives: 19.7 us -> 117 us
  waiting for transfers between devices: 374 us -> 293 us
  local copies, waits for them, and re-layouts: 63.2 us -> 36.5 us
  other arithmetic: 37.4 us -> 12.2 us
  matrix products: 68.6 us -> 59.4 us
    unnamed x5 -> x6, waiting for transfers between devices: 150 us -> 1.44 us
    reduce_scatter x0 -> x2, waiting for transfers between devices: none -> 86.2 us  [the longest x1 52.8 us: on_device(): lax.psum_scatter(terms.reshape(-1, quarter), 'x', scatter_dimension=0, ti...]
    all_to_all x0 -> x2, blocking collectives: none -> 51.1 us  [the longest x1 29.3 us: on_device(): sums = lax.all_to_all(sums.reshape(4, 2, n, quarter), QUAD, 0, 0)]
    psum x1, blocking collectives: 19.7 us -> 66 us  [on_device(): square = lax.psum(square, PLANE)]
    unnamed x27 -> x25, local copies, waits for them, and re-layouts: 37.8 us -> 6.8 us
    concatenate x1 -> x0, other arithmetic: 26.8 us -> none  [on_device(): jnp.concatenate([contract_rows(tokens, slope_two), contract_rows(cotangen...]
    all_gather x2 -> x0, local copies, waits for them, and re-layouts: 25.4 us -> none  [the longest x1 12.8 us: on_device(): lax.all_gather(w_out, 'fsdp', axis=1, tiled=True)]
    psum x1, waiting for transfers between devices: 83.7 us -> 62 us  [on_device(): input_grad = lax.psum(share, ('z', 'ylo'))]
  transfers between devices with their start and end apart: 4 -> 6, of which waited for: 4 -> 6; matrix products, arithmetic and copies ran while one was open for 5% -> 8% of each run, Pallas kernels for 0% -> 0%
where the time goes in v1:
time: 533 us; the launch traced here: 532 us
  waiting for transfers between devices  293 us (55%)
  blocking collectives  117 us (22%)
  matrix products  59.4 us (11%)
  local copies, waits for them, and re-layouts  36.5 us (7%)
  between operations  14.3 us (3%)
  other arithmetic  12.2 us (2%)
    psum x1, blocking collectives, on_device(): square = lax.psum(square, PLANE)  66 us
    psum x1, waiting for transfers between devices, on_device(): input_grad = lax.psum(share, ('z', 'ylo'))  62 us
    reduce_scatter x1, waiting for transfers between devices, on_device(): lax.psum_scatter(terms.reshape(-1, quarter), 'x', scatter_dimension=0, ti...  52.8 us
    all_gather x1, waiting for transfers between devices, on_device(): full = lax.all_gather(mine, 'x', axis=0)  51.1 us
    all_gather x1, waiting for transfers between devices, on_device(): cot = lax.all_gather(cotangent, QUAD, axis=0, tiled=True)  47.7 us
    all_gather x1, waiting for transfers between devices, on_device(): tok = lax.all_gather(tokens, QUAD, axis=0, tiled=True)  44.1 us
    reduce_scatter x1, waiting for transfers between devices, on_device(): lax.psum_scatter(partial.astype(jnp.bfloat16), QUAD, scatter_dimension=0,...  33.3 us
    all_to_all x1, blocking collectives, on_device(): sums = lax.all_to_all(sums.reshape(4, 2, n, quarter), QUAD, 0, 0)  29.3 us
  transfers between devices with their start and end apart: 6, of which 6 were waited for; matrix products, arithmetic and copies ran while one was open for 8% of the time, Pallas kernels for 0%

profile of v1, /device:TPU:0, one launch (start us, length us, event | category | flops | bytes accessed | tf_op | source)
XLA Modules:
  0.0 532.3 jit_solution(8730133469661230747)
XLA Ops:
  10.0 21.8 %all_to_all.10 = bf16[4,2,192,384]{3,2,1,0:T(8,128)(2,1)} all-to-all(bf16[4,2,192,384]{3,2,1,0:T(8,128)(2,1)S(1)} %copy.61), channel_id=1, replica_groups=mesh['z'=4,'ylo'=2,'yhi'=2,'x'=4,'core'=2] {'yhi','core'}, dimensions={0} | all-to-all | bytes 2359296 | tf_op jit(solution)/shard_map/all_to_all | solution.py:48
  33.4 51.1 %all-gather.9.cloned.1.call-done = bf16[16,2,192,384]{3,2,1,0:T(8,128)(2,1)} async-done(((bf16[4,2,192,384]{3,2,1,0:T(8,128)(2,1)}), bf16[16,2,192,384]{3,2,1,0:T(8,128)(2,1)}) %all-gather.9.cloned.1.call-update) | async-done | bytes 4718608 | tf_op jit(solution)/shard_map/all_gather | solution.py:49
  84.5 2.9 fusion.28
  89.4 47.7 %all-gather.5.cloned.1.call-done = bf16[1024,3072]{1,0:T(8,128)(2,1)} async-done(((bf16[256,3072]{1,0:T(8,128)(2,1)}), bf16[1024,3072]{1,0:T(8,128)(2,1)}) %all-gather.5.cloned.1.call-update) | async-done | bytes 6291472 | tf_op jit(solution)/shard_map/all_gather | solution.py:43
  137.1 7.4 %fusion.32 = f32[4,256,256]{2,1,0:T(8,128)} fusion(bf16[4,256,3072]{2,1,0:T(8,128)(2,1)} %bitcast.116), kind=kOutput, calls=%fused_computation.56 | convolution fusion | flops 1610612736 | bytes 7340032 | tf_op jit(solution)/shard_map/gtd,gud->gtu/dot_general | solution.py:32
  144.5 44.1 %all-gather.7.cloned.1.call-done = bf16[1024,3072]{1,0:T(8,128)(2,1)} async-done(((bf16[256,3072]{1,0:T(8,128)(2,1)}), bf16[1024,3072]{1,0:T(8,128)(2,1)}) %all-gather.7.cloned.1.call-update) | async-done | bytes 6291472 | tf_op jit(solution)/shard_map/all_gather | solution.py:42
  188.6 7.5 %fusion.31 = f32[4,256,256]{2,1,0:T(8,128)} fusion(bf16[4,256,3072]{2,1,0:T(8,128)(2,1)} %bitcast.105), kind=kOutput, calls=%fused_computation.55 | convolution fusion | flops 1610612736 | bytes 7340032 | tf_op jit(solution)/shard_map/gtd,gud->gtu/dot_general | solution.py:32
  198.9 4.6 fusion.18
  211.9 66.0 %psum.14 = f32[4]{0:T(128)S(1)} all-reduce(f32[4]{0:T(128)S(1)} %add.45), channel_id=1, replica_groups=mesh['z'=4,'ylo'=2,'yhi'=2,'x'=4,'core'=2] {'z','ylo','yhi','core'}, use_global_device_ids=true, to_apply=%region_2.0 | all-reduce | flops 4 | bytes 32 | tf_op jit(solution)/shard_map/psum | solution.py:63
  277.9 4.0 broadcast_multiply_fusion.1
  281.9 3.0 copy.79
  284.9 3.0 copy.80
  288.0 4.5 fusion.14
  294.8 9.7 %fusion.20 = f32[4,256,3072]{2,1,0:T(8,128)} fusion(bf16[4,256,3072]{2,1,0:T(8,128)(2,1)} %bitcast.106, bf16[4,256,384]{2,1,0:T(8,128)(2,1)} %bitcast.110, bf16[4,256,384]{2,1,0:T(8,128)(2,1)S(1)} %bitcast.96, f32[4]{0:T(128)S(1)} %rsqrt_multiply_fusion), kind=kOutput, calls=%fused_computation.38 | convolution fusion | flops 1812463616 | bytes 20447248 | tf_op jit(solution)/shard_map/gtu,gud->gtd/dot_general | solution.py:74
  304.5 8.4 %fusion = bf16[1024,3072]{1,0:T(8,128)(2,1)} fusion(f32[4,256,3072]{2,1,0:T(8,128)} %fusion.20, bf16[1024,384]{0,1:T(8,128)(2,1)} %fusion.14, bf16[3072,384]{1,0:T(8,128)(2,1)S(1)} %bitcast.98), kind=kOutput, calls=%fused_computation.1 | convolution fusion | flops 2422210560 | bytes 22020096 | tf_op jit(solution)/shard_map/dot_general | solution.py:20
  314.7 6.8 %fusion.2 = bf16[3072,384]{0,1:T(8,128)(2,1)} fusion(bf16[1024,3072]{1,0:T(8,128)(2,1)} %all-gather.5.cloned.1.call-done, f32[1024,384]{0,1:T(8,128)S(1)} %copy-done.2, f32[384,1024]{1,0:T(8,128)S(1)} %copy-done.7), kind=kOutput, calls=%fused_computation.6 | convolution fusion | flops 2419458048 | bytes 11796480 | tf_op jit(solution)/shard_map/dot_general | solution.py:20
  321.5 3.3 copy.73
  324.8 6.8 %fusion.1 = bf16[3072,384]{0,1:T(8,128)(2,1)} fusion(bf16[1024,384]{0,1:T(8,128)(2,1)S(1)} %copy-done, bf16[1024,3072]{1,0:T(8,128)(2,1)} %all-gather.7.cloned.1.call-done), kind=kOutput, calls=%fused_computation.5 | convolution fusion | flops 2417098752 | bytes 9437184 | tf_op jit(solution)/shard_map/dot_general | solution.py:20
  331.6 4.3 copy.72
  335.9 2.7 maximum_bitcast_fusion
  341.2 33.3 %reduce-scatter.5.cloned.1.call-done = bf16[256,3072]{1,0:T(8,128)(2,1)} async-done(((bf16[1024,3072]{1,0:T(8,128)(2,1)}), bf16[256,3072]{1,0:T(8,128)(2,1)}) %reduce-scatter.5.cloned.1.call-update) | async-done | bytes 1572880 | tf_op jit(solution)/shard_map/reduce_scatter | solution.py:76
  374.6 52.8 %reduce-scatter.3.cloned.1.call-done = bf16[1536,384]{1,0:T(8,128)(2,1)} async-done(((bf16[6144,384]{1,0:T(8,128)(2,1)}), bf16[1536,384]{1,0:T(8,128)(2,1)}) %reduce-scatter.3.cloned.1.call-update) | async-done | bytes 1179664 | tf_op jit(solution)/shard_map/reduce_scatter | solution.py:80
  427.4 29.3 %all_to_all.11 = bf16[4,2,192,384]{3,2,1,0:T(8,128)(2,1)S(1)} all-to-all(bf16[4,2,192,384]{3,2,1,0:T(8,128)(2,1)} %bitcast.112), channel_id=1, replica_groups=mesh['z'=4,'ylo'=2,'yhi'=2,'x'=4,'core'=2] {'yhi','core'}, dimensions={0} | all-to-all | bytes 2359296 | tf_op jit(solution)/shard_map/all_to_all | solution.py:81
  460.8 62.0 %all-reduce.2.cloned.1.call-done = bf16[256,3072]{1,0:T(8,128)(2,1)} async-done(((bf16[256,3072]{1,0:T(8,128)(2,1)}), bf16[256,3072]{1,0:T(8,128)(2,1)}) %all-reduce.2.cloned.1.call-update) | async-done | bytes 1572880 | tf_op jit(solution)/shard_map/psum | solution.py:77
  (58 shorter events, 30.9 us)
Async XLA Ops:
  7.2 1.7 copy-start.9
  7.2 77.3 %all-gather.9.cloned.1.call-start = ((), (), s32[]{:S(2)}) async-start(), calls=%async_computation.9 | async-start | bytes 5898240 | tf_op jit(solution)/shard_map/all_gather | solution.py:49
  31.9 105.2 %all-gather.5.cloned.1.call-start = ((), (), s32[]{:S(2)}) async-start(), calls=%async_computation.4 | async-start | bytes 7864320 | tf_op jit(solution)/shard_map/all_gather | solution.py:43
  32.6 156.0 %all-gather.7.cloned.1.call-start = ((), (), s32[]{:S(2)}) async-start(), calls=%async_computation.5 | async-start | bytes 7864320 | tf_op jit(solution)/shard_map/all_gather | solution.py:42
  33.4 341.2 %reduce-scatter.5.cloned.1.call-start = ((), (), s32[]{:S(2)}) async-start(), calls=%async_computation.7 | async-start | bytes 7864320 | tf_op jit(solution)/shard_map/reduce_scatter | solution.py:76
  188.6 7.5 %copy-start.6 = (bf16[1,2,4,2,192,384]{5,4,3,2,1,0:T(8,128)(2,1)S(1)}, bf16[1,2,4,2,192,384]{5,4,3,2,1,0:T(8,128)(2,1)}, u32[]{:S(2)}) copy-start(bf16[1,2,4,2,192,384]{5,4,3,2,1,0:T(8,128)(2,1)} %copy.62) | copy-start | bytes 7077892
  188.6 7.5 %copy-start.10 = (bf16[1024,3072]{1,0:T(8,128)(2,1)S(1)}, bf16[1024,3072]{1,0:T(8,128)(2,1)}, u32[]{:S(2)}) copy-start(bf16[1024,3072]{1,0:T(8,128)(2,1)} %all-gather.5.cloned.1.call-done) | copy-start | bytes 18874372
  196.2 2.8 copy-start.3
  198.8 4.8 copy-start.8
  206.2 1.8 copy-start.5
  208.0 1.7 copy-start.1
  208.0 1.6 copy-start.4
  312.9 1.4 copy-start.2
  312.9 1.9 copy-start.7
  312.9 114.5 %reduce-scatter.3.cloned.1.call-start = ((), (), s32[]{:S(2)}) async-start(), calls=%async_computation.6 | async-start | bytes 5898240 | tf_op jit(solution)/shard_map/reduce_scatter | solution.py:80
  321.5 3.3 copy-start
  341.2 181.6 %all-reduce.2.cloned.1.call-start = ((), (), s32[]{:S(2)}) async-start(), calls=%async_computation.8 | async-start | bytes 3145728 | tf_op jit(solution)/shard_map/psum | solution.py:77
Sparse Core Ops, SparseCore 0:
  32.0 52.4 all-gather.8
  86.2 50.8 all-gather.4
  138.7 49.8 all-gather.6
  313.0 61.5 reduce-scatter.4
  377.0 50.4 reduce-scatter.2
  430.0 92.8 all-reduce.1

commit v2 on v0

v2 whole, which is shorter than its diff:
```python
import math

import jax
import jax.numpy as jnp
from jax import lax
from jax.experimental import pallas as pl
from jax.experimental.pallas import tpu as pltpu
from jax.sharding import PartitionSpec as P

D = 3072
FF = 12288
TOKENS = 4096
GROUP = 256
ROWS = 192
QUARTER = 384
HALF = 1536

RADIUS_SHARE = 0.5
EPSILON = 1e-06
BF = jnp.bfloat16
F32 = jnp.float32
MESH = pl.DeviceIdType.MESH


def dot(a, b, dims):
    return lax.dot_general(a, b, (dims, ((), ())), preferred_element_type=F32)


def gelu_pair(h):
    cdf = 0.5 * (1.0 + lax.erf(h * (1.0 / math.sqrt(2.0))))
    pdf = jnp.exp(-0.5 * h * h) * (1.0 / math.sqrt(2.0 * math.pi))
    return h * cdf, cdf + h * pdf


def kernel(
    tok_ref, cot_ref, w2_ref, quad_out, input_out,
    X, W, HB, GS, GM, S1, S2, T, HOP, FL, FR, OS, PO, PS, PR, YB, ZA, RA, RB, YA, ZB, IG,
    SQ, SQR, FAC, send, recv, local,
):
    dp, fs = lax.axis_index("dp"), lax.axis_index("fsdp")
    z, ylo = dp // 2, lax.rem(dp, 2)
    yhi, x, c = fs // 8, lax.rem(fs // 2, 4), lax.rem(fs, 2)

    def dev(z, ylo, yhi, x, c):
        return (z * 2 + ylo, yhi * 8 + x * 2 + c)

    right, left, across = lax.rem(x + 1, 4), lax.rem(x + 3, 4), lax.rem(x + 2, 4)
    z_up, z_down, z_far = lax.rem(z + 1, 4), lax.rem(z + 3, 4), lax.rem(z + 2, 4)
    to_sib = dev(z, ylo, yhi, x, 1 - c)
    to_quad = [None, to_sib, dev(z, ylo, 1 - yhi, x, c), dev(z, ylo, 1 - yhi, x, 1 - c)]
    to_right, to_left = dev(z, ylo, yhi, right, c), dev(z, ylo, yhi, left, c)
    to_z = [dev(zz, ylo, yhi, x, c) for zz in (z_up, z_down, z_far)]
    to_yn, to_ym, to_y2 = dev(z, 1 - ylo, 1 - yhi, x, c), dev(z, 1 - ylo, yhi, x, c), to_quad[2]
    to_y = [to_ym, to_yn, to_y2]
    y_of = [(yhi, 1 - ylo), (1 - yhi, 1 - ylo), (1 - yhi, ylo)]
    z_of = [z_up, z_down, z_far]

    count = [0]
    pending = []

    def remote(src, dst, target, keep=True):
        i = count[0]
        count[0] += 1
        copy = pltpu.make_async_remote_copy(
            src_ref=src, dst_ref=dst, send_sem=send.at[i], recv_sem=recv.at[i],
            device_id=target, device_id_type=MESH,
        )
        copy.start()
        if keep:
            pending.append(copy)
        return copy

    member = [(yhi, c), (yhi, 1 - c), (1 - yhi, c), (1 - yhi, 1 - c)]

    def rows_of(xx, j):
        yy, cc = member[j]
        return pl.ds(pl.multiple_of((yy * 8 + xx * 2 + cc) * ROWS, 64), ROWS)

    def quarter_of(j):
        yy, cc = member[j]
        return pl.ds(pl.multiple_of((yy * 2 + cc) * QUARTER, 128), QUARTER)

    def group_rows(j, start=0, size=GROUP):
        yy, cc = member[j]
        return pl.ds(pl.multiple_of((yy * 2 + cc) * GROUP + start, 64), size)

    barrier = pltpu.get_barrier_semaphore()
    peers = [to_sib, to_quad[2], to_quad[3], to_right, to_left, *to_z, to_yn, to_ym]
    copies = [
        pltpu.make_async_copy(tok_ref, X.at[0, group_rows(0)], local.at[0]),
        pltpu.make_async_copy(cot_ref, X.at[1, group_rows(0)], local.at[1]),
        pltpu.make_async_copy(w2_ref.at[:, :, quarter_of(0)], W.at[:, rows_of(x, 0)], local.at[2]),
    ]
    for copy in copies:
        copy.start()
    for peer in peers:
        pl.semaphore_signal(barrier, inc=1, device_id=peer, device_id_type=MESH)
    pl.semaphore_wait(barrier, len(peers))

    quad = [None] + [
        remote(w2_ref.at[:, :, quarter_of(j)], W.at[:, rows_of(x, 0)], to_quad[j]) for j in (2, 3, 1)
    ]
    quad = [None, quad[3], quad[1], quad[2]]
    from_left, from_right = [None] * 4, [None] * 4

    def ring(j):
        block = W.at[:, rows_of(x, j)]
        from_left[j] = remote(block, block, to_right)
        from_right[j] = remote(block, block, to_left)

    def relay_right(j):
        from_left[j].wait_recv()
        block = W.at[:, rows_of(left, j)]
        return remote(block, block, to_right)

    def relay_left(j):
        from_right[j].wait_recv()
        block = W.at[:, rows_of(right, j)]
        return remote(block, block, to_left)

    for copy in copies:
        copy.wait()
    ring(0)
    slice_rows = lambda zz: group_rows(0, zz * 64, 64)
    part_rows = lambda zz: group_rows(2, zz * 64, 64)
    tok_y = [remote(X.at[k, slice_rows(z)], X.at[k, slice_rows(z)], to_yn) for k in (0, 1)]
    tok_c = [remote(X.at[k, group_rows(0)], X.at[k, group_rows(0)], to_sib) for k in (0, 1)]

    def gram(k, rows):
        block = X[k, rows, :]
        g = dot(block, block, ((1,), (1,)))
        hi = g.astype(BF)
        GM[k, 0, rows, :] = hi
        GM[k, 1, rows, :] = (g - hi.astype(F32)).astype(BF)

    def gram_of(j):
        @pl.loop(0, 2)
        def _(k):
            gram(k, group_rows(j))

    quad[1].wait_recv()
    ring(1)
    gram_of(0)
    relays = [relay_right(0), relay_left(1)]
    for copy in tok_c:
        copy.wait_recv()
    gram_of(1)
    tok_up, tok_down, tok_far, tok_fwd = [None] * 2, [None] * 2, [None] * 2, []

    def forward(k, zz):
        block = X.at[k, part_rows(zz)]
        tok_fwd.append(remote(block, block, to_sib))

    def spread(k):
        tok_y[k].wait_recv()
        block = X.at[k, part_rows(z)]
        tok_up[k] = remote(block, block, to_z[0])
        tok_down[k] = remote(block, block, to_z[1])
        forward(k, z)

    spread(0)
    quad[2].wait_recv()
    ring(2)
    quad[3].wait_recv()
    ring(3)
    spread(1)
    tok_up[0].wait_recv()
    block = X.at[0, part_rows(z_down)]
    tok_far[0] = remote(block, block, to_z[0])
    forward(0, z_down)
    tok_down[0].wait_recv()
    forward(0, z_up)
    relays += [relay_right(2)]
    tok_down[1].wait_recv()
    block = X.at[1, part_rows(z_up)]
    tok_far[1] = remote(block, block, to_z[1])
    forward(1, z_up)
    tok_up[1].wait_recv()
    forward(1, z_down)
    relays += [relay_left(3)]
    for k in (0, 1):
        tok_far[k].wait_recv()
        forward(k, z_far)
    for copy in tok_fwd:
        copy.wait_recv()
    gram_of(2)
    gram_of(3)
    for j in (1, 3):
        from_left[j].wait_recv()
    for j in (0, 2):
        from_right[j].wait_recv()
    for copy in relays:
        copy.wait_recv()

    SQ[...] = jnp.zeros_like(SQ)

    @pl.loop(0, 4)
    def _(g):
        rows = pl.ds(pl.multiple_of(g * GROUP, GROUP), GROUP)

        @pl.loop(0, 2)
        def _(k):
            HB[k, rows, :] = dot(X[k, rows, :], W[k], ((1,), (0,)))

        @pl.loop(0, 4)
        def _(s):
            part = pl.ds(pl.multiple_of(g * GROUP + s * 64, 64), 64)
            act, der = gelu_pair(HB[0, part, :])
            S1[0, part, :] = (HB[1, part, :] * der).astype(BF)
            S1[1, part, :] = act.astype(BF)

        @pl.loop(0, 2)
        def _(k):
            s = S1[k, rows, :]
            gs = dot(GM[k, 0, rows, :], s, ((1,), (0,))) + dot(GM[k, 1, rows, :], s, ((1,), (0,)))
            GS[k, rows, :] = gs
            row = jnp.sum(gs * s.astype(F32), axis=0, keepdims=True)
            row = row[:, :128] + row[:, 128:256] + row[:, 256:]
            SQ[pl.ds(g, 1), :] += row

    def exchange(slot, targets):
        got = [remote(SQ, SQR.at[slot + i], t, keep=False) for i, t in enumerate(targets)]
        for copy in got:
            copy.wait_recv()
            copy.wait_send()
        total = SQ[...]
        for i in range(len(targets)):
            total += SQR[slot + i]
        SQ[...] = total

    exchange(0, [to_sib])
    exchange(1, to_y)
    exchange(4, to_z)
    square = jnp.sum(SQ[...], axis=1, keepdims=True)
    FAC[...] = jnp.broadcast_to(RADIUS_SHARE * math.sqrt(D + FF) / jnp.sqrt(square + EPSILON), FAC.shape)

    @pl.loop(0, 16)
    def _(s):
        part = pl.ds(pl.multiple_of(s * 64, 64), 64)
        f = FAC[pl.ds(s // 4, 1), :][:, :1]
        act, der = gelu_pair(HB[0, part, :] + f * GS[0, part, :])
        S2[0, part, :] = ((HB[1, part, :] + f * GS[1, part, :]) * der).astype(BF)
        S2[1, part, :] = act.astype(BF)

    def term(xx, dy):
        yy = yhi if dy == 0 else 1 - yhi
        base = pl.ds(pl.multiple_of((yy * 4 + xx) * QUARTER, 128), QUARTER)

        @pl.loop(0, 2)
        def _(k):
            T[k, base, :] = dot(X[k, :, base], S2[k], ((0,), (0,))).astype(BF)

    def send_term(src_x, j, dst, target):
        return remote(T.at[:, rows_of(src_x, j)], dst, target)

    hop = [None] * 4
    term(across, 1)
    hop[2] = send_term(across, 2, HOP.at[2], to_right)
    hop[3] = send_term(across, 3, HOP.at[3], to_left)
    term(across, 0)
    hop[0] = send_term(across, 0, HOP.at[0], to_right)
    hop[1] = send_term(across, 1, HOP.at[1], to_left)

    def input_rows(yy, cc, dst, add):
        g = yy * 2 + cc
        rows = pl.ds(pl.multiple_of(g * GROUP, GROUP), GROUP)
        f = FAC[pl.ds(g, 1), :][:, :1]
        cross = (f * dot(S2[0, rows, :], S1[0, rows, :], ((1,), (1,)))).astype(BF)

        @pl.loop(0, 4)
        def _(n):
            cols = pl.ds(pl.multiple_of(n * 768, 768), 768)
            out = dot(S2[0, rows, :], W[0, cols, :], ((1,), (1,))) + dot(cross, X[0, rows, cols], ((1,), (0,)))
            out = out.reshape(4, 2, 32, 768)
            if add is not None:
                out = out + add[yy, :, :, :, cols].astype(F32)
            dst[yy, :, :, :, cols] = out.astype(BF)

    to_core = []
    for yy in (0, 1):
        input_rows(yy, 1 - c, PS, None)
        to_core.append(remote(PS.at[yy], PR.at[yy], to_sib))
    final_left, final_right = [None] * 4, [None] * 4
    term(right, 1)
    final_left[3] = send_term(right, 3, FL.at[3], to_right)
    term(left, 1)
    final_right[2] = send_term(left, 2, FR.at[2], to_left)
    for yy in (0, 1):
        to_core[yy].wait_recv()
        input_rows(yy, c, PO, PR)
    lo, hi = pl.ds(0, HALF), pl.ds(HALF, HALF)
    za = [remote(PO.at[:, z_of[i], :, :, lo], ZA.at[i], to_z[i]) for i in range(3)]
    yb = [remote(PO.at[y_of[i][0], :, y_of[i][1], :, hi], YB.at[i], to_y[i]) for i in range(3)]

    def add_hop(xx, j):
        hop[j].wait_recv()
        rows = rows_of(xx, j)
        T[:, rows, :] = (T[:, rows, :].astype(F32) + HOP[j].astype(F32)).astype(BF)

    add_hop(right, 2)
    final_left[2] = send_term(right, 2, FL.at[2], to_right)
    add_hop(left, 3)
    final_right[3] = send_term(left, 3, FR.at[3], to_left)
    term(right, 0)
    final_left[1] = send_term(right, 1, FL.at[1], to_right)
    term(left, 0)
    final_right[0] = send_term(left, 0, FR.at[0], to_left)
    add_hop(right, 0)
    final_left[0] = send_term(right, 0, FL.at[0], to_right)
    add_hop(left, 1)
    final_right[1] = send_term(left, 1, FR.at[1], to_left)
    term(x, 1)
    term(x, 0)

    def total(j):
        final_left[j].wait_recv()
        final_right[j].wait_recv()
        OS[j] = (T[:, rows_of(x, j), :].astype(F32) + FL[j].astype(F32) + FR[j].astype(F32)).astype(BF)

    my_quarter = yhi * 2 + c

    for copy in za:
        copy.wait_recv()

    @pl.loop(0, 4)
    def _(i):
        a, b = i // 2, lax.rem(i, 2)
        s = PO[a, z, b, :, lo].astype(F32)
        for slot in range(3):
            s += ZA[slot, a, b].astype(F32)
        RA[a, b] = s.astype(BF)

    ya = [remote(RA.at[y_of[i][0], y_of[i][1]], YA.at[i], to_y[i]) for i in range(3)]
    for copy in yb:
        copy.wait_recv()

    @pl.loop(0, 4)
    def _(i):
        s = PO[yhi, i, ylo, :, hi].astype(F32)
        for slot in range(3):
            s += YB[slot, i].astype(F32)
        RB[i] = s.astype(BF)

    zb = [remote(RB.at[z_of[i]], ZB.at[i], to_z[i]) for i in range(3)]
    outs = []
    total(2)
    outs.append(remote(OS.at[2], quad_out.at[my_quarter], to_quad[2]))
    total(3)
    outs.append(remote(OS.at[3], quad_out.at[my_quarter], to_quad[3]))
    for copy in ya:
        copy.wait_recv()
    s = RA[yhi, ylo].astype(F32)
    for slot in range(3):
        s += YA[slot].astype(F32)
    IG[z, ylo, :, lo] = s.astype(BF)
    for copy in zb:
        copy.wait_recv()
    s = RB[z].astype(F32)
    for slot in range(3):
        s += ZB[slot].astype(F32)
    IG[z, ylo, :, hi] = s.astype(BF)

    mine = IG.at[z, ylo]
    ig_ym = remote(mine, mine, to_ym)
    ig = [remote(mine, mine, to_z[i]) for i in range(3)]
    total(1)
    outs.append(remote(OS.at[1], quad_out.at[my_quarter], to_quad[1]))
    total(0)
    own = pltpu.make_async_copy(OS.at[0], quad_out.at[my_quarter], local.at[3])
    own.start()
    ig_ym.wait_recv()
    other = IG.at[z, 1 - ylo]
    ig += [remote(other, other, to_z[i]) for i in range(3)]
    for copy in ig:
        copy.wait_recv()
    done = pltpu.make_async_copy(IG, input_out, local.at[4])
    done.start()
    for copy in outs:
        copy.wait_recv()
    own.wait()
    done.wait()
    for copy in pending:
        copy.wait_send()


def on_device(tokens, cotangent, w_in, w_out):
    grad_scale = 1.0 / math.sqrt(TOKENS)
    both = jnp.stack([w_in, w_out.T])
    any_space = pl.BlockSpec(memory_space=pl.ANY)
    vmem = pltpu.VMEM
    sums, input_grad = pl.pallas_call(
        kernel,
        out_shape=(
            jax.ShapeDtypeStruct((4, 2, ROWS, QUARTER), BF),
            jax.ShapeDtypeStruct((4, 2, 32, D), BF),
        ),
        in_specs=[any_space, any_space, pl.BlockSpec(memory_space=pltpu.VMEM)],
        out_specs=(any_space, any_space),
        scratch_shapes=[
            vmem((2, 4 * GROUP, D), BF),
            vmem((2, D, QUARTER), BF),
            vmem((2, 4 * GROUP, QUARTER), F32),
            vmem((2, 4 * GROUP, QUARTER), F32),
            vmem((2, 2, 4 * GROUP, GROUP), BF),
            vmem((2, 4 * GROUP, QUARTER), BF),
            vmem((2, 4 * GROUP, QUARTER), BF),
            vmem((2, D, QUARTER), BF),
            vmem((4, 2, ROWS, QUARTER), BF),
            vmem((4, 2, ROWS, QUARTER), BF),
            vmem((4, 2, ROWS, QUARTER), BF),
            vmem((4, 2, ROWS, QUARTER), BF),
            vmem((2, 4, 2, 32, D), BF),
            vmem((2, 4, 2, 32, D), BF),
            vmem((2, 4, 2, 32, D), BF),
            vmem((3, 4, 32, HALF), BF),
            vmem((3, 2, 2, 32, HALF), BF),
            vmem((2, 2, 32, HALF), BF),
            vmem((4, 32, HALF), BF),
            vmem((3, 32, HALF), BF),
            vmem((3, 32, HALF), BF),
            vmem((4, 2, 32, D), BF),
            vmem((8, 128), F32),
            vmem((7, 8, 128), F32),
            vmem((8, 128), F32),
            pltpu.SemaphoreType.DMA((96,)),
            pltpu.SemaphoreType.DMA((96,)),
            pltpu.SemaphoreType.DMA((5,)),
        ],
        compiler_params=pltpu.CompilerParams(
            collective_id=0, has_side_effects=True, vmem_limit_bytes=63 * 2**20
        ),
        cost_estimate=pl.CostEstimate(flops=20 * 10**9, bytes_accessed=40 * 2**20, transcendentals=10**6),
    )(tokens, cotangent, both)
    grads = sums.transpose(1, 2, 0, 3).reshape(2, ROWS, 4 * QUARTER).astype(F32) * grad_scale
    return grads[0], grads[1].T, input_grad.reshape(GROUP, D)


def solution(mesh):
    return jax.shard_map(
        on_device,
        mesh=mesh,
        in_specs=(P("fsdp", None), P("fsdp", None), P("fsdp", "dp"), P("dp", "fsdp")),
        out_specs=(P("fsdp", "dp"), P("dp", "fsdp"), P("fsdp", None)),
        check_vma=False,
    )
```

time: 580 us -> 158 us (0.27)
  waiting for transfers between devices: 374 us -> 0 us
  Pallas kernels: 0 us -> 147 us
  matrix products: 68.6 us -> 0 us
  local copies, waits for them, and re-layouts: 63.2 us -> 5.74 us
  other arithmetic: 37.4 us -> 3.8 us
  blocking collectives: 19.7 us -> 0 us
  between operations: 15.9 us -> 0.67 us
    unnamed x5 -> x0, waiting for transfers between devices: 150 us -> none
    pallas_call x0 -> x1, Pallas kernels: none -> 147 us  [on_device(): pl.pallas_call(kernel, out_shape=(jax.ShapeDtypeStruct((4, 2, ROWS, QUART...]
    all_gather x2 -> x0, waiting for transfers between devices: 140 us -> none  [the longest x1 81.3 us: on_device(): lax.all_gather(w_in, 'fsdp', axis=0, tiled=True)]
    psum x1 -> x0, waiting for transfers between devices: 83.7 us -> none  [on_device(): input_grad = lax.psum(partial_input.astype(jnp.bfloat16), 'dp')]
    dot_general x9 -> x0, matrix products: 68.6 us -> none  [the longest x4 34.6 us: contract_rows(): lax.dot_general(first_op, second_op, (((0,), (0,)), ((), ())), preferred_...]
    unnamed x27 -> x5, local copies, waits for them, and re-layouts: 37.8 us -> 4.06 us
    concatenate x1 -> x0, other arithmetic: 26.8 us -> none  [on_device(): jnp.concatenate([contract_rows(tokens, slope_two), contract_rows(cotangen...]
    all_gather x2 -> x0, local copies, waits for them, and re-layouts: 25.4 us -> none  [the longest x1 12.8 us: on_device(): lax.all_gather(w_out, 'fsdp', axis=1, tiled=True)]
  transfers between devices with their start and end apart: 4 -> 0, of which waited for: 4 -> 0; matrix products, arithmetic and copies ran while one was open for 5% -> 0% of each run, Pallas kernels for 0% -> 0%
where the time goes in v2:
time: 158 us
  Pallas kernels  147 us (93%)
  local copies, waits for them, and re-layouts  5.74 us (4%)
  other arithmetic  3.8 us (2%)
    pallas_call x1, Pallas kernels, on_device(): pl.pallas_call(kernel, out_shape=(jax.ShapeDtypeStruct((4, 2, ROWS, QUART...  147 us
    unnamed x5, local copies, waits for them, and re-layouts  4.06 us

profile of v2, /device:TPU:0, one launch (start us, length us, event | category | flops | bytes accessed | tf_op | source)
XLA Modules:
  0.0 157.6 jit_solution(10557740734525513435)
XLA Ops:
  0.6 2.4 %pad_maximum_fusion.w2_ref = bf16[2,192,1536]{2,1,0:T(8,128)(2,1)} fusion(bf16[1,192,1536]{2,1,0:T(8,128)(2,1)} %bitcast.20, bf16[1,192,1536]{2,1,0:T(8,128)(2,1)} %bitcast.21), kind=kLoop, calls=%fused_computation.1 | loop fusion | flops 589824 | bytes 2359296 | tf_op jit(solution)/shard_map/stack | solution.py:388
  3.0 147.4 %shard_map.67 = (bf16[4,2,192,384]{3,2,1,0:T(8,128)(2,1)}, bf16[4,2,32,3072]{3,2,1,0:T(8,128)(2,1)}) custom-call(bf16[256,3072]{1,0:T(8,128)(2,1)} %tok_ref.1, bf16[256,3072]{1,0:T(8,128)(2,1)} %cot_ref.1, bf16[2,192,1536]{2,1,0:T(8,128)(2,1)} %pad_maximum_fusion.w2_ref), custom_call_target="tpu_custom_call" | custom-call | flops 20000000000 | bytes 41943040 | tf_op jit(solution)/shard_map/pallas_call | solution.py:391
  150.4 1.4 multiply_bitcast_fusion
  151.8 0.2 fusion
  152.0 0.8 copy.8
  152.8 1.1 copy.10
  153.9 0.8 copy.7
  154.6 0.0 copy-start
  154.6 1.1 copy.9
  155.7 0.7 copy-done
  156.5 1.1 copy.12
Async XLA Ops:
  154.6 1.8 %copy-start = (bf16[4,2,32,3072]{3,2,1,0:T(8,128)(2,1)S(1)}, bf16[4,2,32,3072]{3,2,1,0:T(8,128)(2,1)}, u32[]{:S(2)}) copy-start(bf16[4,2,32,3072]{3,2,1,0:T(8,128)(2,1)} %get-tuple-element.6) | copy-start | bytes 4718596

commit v3 on v2

v3 whole, which is shorter than its diff:
```python
import math

import jax
import jax.numpy as jnp
from jax import lax
from jax.experimental import pallas as pl
from jax.experimental.pallas import tpu as pltpu
from jax.sharding import PartitionSpec as P

D = 3072
FF = 12288
TOKENS = 4096
GROUP = 256
ROWS = 192
QUARTER = 384
HALF = 1536

RADIUS_SHARE = 0.5
EPSILON = 1e-06
BF = jnp.bfloat16
F32 = jnp.float32
MESH = pl.DeviceIdType.MESH


def dot(a, b, dims):
    return lax.dot_general(a, b, (dims, ((), ())), preferred_element_type=F32)


def gelu_pair(h):
    cdf = 0.5 * (1.0 + lax.erf(h * (1.0 / math.sqrt(2.0))))
    pdf = jnp.exp(-0.5 * h * h) * (1.0 / math.sqrt(2.0 * math.pi))
    return h * cdf, cdf + h * pdf


def kernel(
    tok_ref, cot_ref, win_ref, wout_ref, gin_out, gout_out, input_out,
    X, W, HB, GS, GM, S1, S2, T, HOP, FL, FR, OS, PO, PS, PR, ZH, ZF, YB, RA, RB, YA, ZB, IG,
    SQ, SQR, FAC, send, recv, local,
):
    dp, fs = lax.axis_index("dp"), lax.axis_index("fsdp")
    z, ylo = dp // 2, lax.rem(dp, 2)
    yhi, x, c = fs // 8, lax.rem(fs // 2, 4), lax.rem(fs, 2)

    def dev(z, ylo, yhi, x, c):
        return (z * 2 + ylo, yhi * 8 + x * 2 + c)

    right, left, across = lax.rem(x + 1, 4), lax.rem(x + 3, 4), lax.rem(x + 2, 4)
    z_up, z_down, z_far = lax.rem(z + 1, 4), lax.rem(z + 3, 4), lax.rem(z + 2, 4)
    to_sib = dev(z, ylo, yhi, x, 1 - c)
    to_quad = [None, to_sib, dev(z, ylo, 1 - yhi, x, c), dev(z, ylo, 1 - yhi, x, 1 - c)]
    to_right, to_left = dev(z, ylo, yhi, right, c), dev(z, ylo, yhi, left, c)
    to_z = [dev(zz, ylo, yhi, x, c) for zz in (z_up, z_down, z_far)]
    to_yn, to_ym, to_y2 = dev(z, 1 - ylo, 1 - yhi, x, c), dev(z, 1 - ylo, yhi, x, c), to_quad[2]
    to_y = [to_ym, to_yn, to_y2]
    y_of = [(yhi, 1 - ylo), (1 - yhi, 1 - ylo), (1 - yhi, ylo)]
    z_of = [z_up, z_down, z_far]

    count = [0]
    pending = []

    def remote(src, dst, target, keep=True):
        i = count[0]
        count[0] += 1
        copy = pltpu.make_async_remote_copy(
            src_ref=src, dst_ref=dst, send_sem=send.at[i], recv_sem=recv.at[i],
            device_id=target, device_id_type=MESH,
        )
        copy.start()
        if keep:
            pending.append(copy)
        return copy

    member = [(yhi, c), (yhi, 1 - c), (1 - yhi, c), (1 - yhi, 1 - c)]

    def rows_of(xx, j):
        yy, cc = member[j]
        return pl.ds(pl.multiple_of((yy * 8 + xx * 2 + cc) * ROWS, 64), ROWS)

    def quarter_of(j):
        yy, cc = member[j]
        return pl.ds(pl.multiple_of((yy * 2 + cc) * QUARTER, 128), QUARTER)

    def group_rows(j, start=0, size=GROUP):
        yy, cc = member[j]
        return pl.ds(pl.multiple_of((yy * 2 + cc) * GROUP + start, 32), size)

    barrier = pltpu.get_barrier_semaphore()
    peers = [to_sib, to_quad[2], to_quad[3], to_right, to_left, *to_z, to_yn, to_ym]
    tokens_of, weights_of = (tok_ref, cot_ref), (win_ref, wout_ref)
    copies = [
        pltpu.make_async_copy(weights_of[k].at[:, quarter_of(0)], W.at[k, rows_of(x, 0)], local.at[k])
        for k in (0, 1)
    ] + [pltpu.make_async_copy(tokens_of[k], X.at[k, group_rows(0)], local.at[2 + k]) for k in (0, 1)]
    for copy in copies:
        copy.start()
    for peer in peers:
        pl.semaphore_signal(barrier, inc=1, device_id=peer, device_id_type=MESH)
    pl.semaphore_wait(barrier, len(peers))

    quad = [None] * 4

    def to_member(j):
        quad[j] = [
            remote(weights_of[k].at[:, quarter_of(j)], W.at[k, rows_of(x, 0)], to_quad[j]) for k in (0, 1)
        ]

    def to_partner(k):
        rows = pl.ds(pl.multiple_of(z * 64 + ylo * 32, 32), 32)
        return remote(tokens_of[k].at[rows], X.at[k, group_rows(0, z * 64 + ylo * 32, 32)], to_yn)

    tok_n = [to_partner(k) for k in (0, 1)]
    to_member(1)
    from_left, from_right = [None] * 4, [None] * 4

    def ring(j):
        block = W.at[:, rows_of(x, j)]
        from_left[j] = remote(block, block, to_right)
        from_right[j] = remote(block, block, to_left)

    def relay_right(j):
        from_left[j].wait_recv()
        block = W.at[:, rows_of(left, j)]
        return remote(block, block, to_right)

    def relay_left(j):
        from_right[j].wait_recv()
        block = W.at[:, rows_of(right, j)]
        return remote(block, block, to_left)

    for copy in copies[:2]:
        copy.wait()
    ring(0)
    for copy in copies[2:]:
        copy.wait()
    tok_c = [remote(X.at[k, group_rows(0)], X.at[k, group_rows(0)], to_sib) for k in (0, 1)]

    def got(copies):
        for copy in copies:
            copy.wait_recv()

    def gram_of(j):
        @pl.loop(0, 2)
        def _(k):
            rows = group_rows(j)
            block = X[k, rows, :]
            g = dot(block, block, ((1,), (1,)))
            hi = g.astype(BF)
            GM[k, 0, rows, :] = hi
            GM[k, 1, rows, :] = (g - hi.astype(F32)).astype(BF)

    def hidden(yy, xx, first=False):
        @pl.loop(0, 4)
        def _(i):
            k = i // 2
            rows = pl.ds(pl.multiple_of((yy * 2 + lax.rem(i, 2)) * GROUP, GROUP), GROUP)
            out = None
            for half in (0, 1):
                base = pl.ds(pl.multiple_of((half * 4 + xx) * QUARTER, 128), QUARTER)
                part = dot(X[k, rows, base], W[k, base, :], ((1,), (0,)))
                out = part if out is None else out + part
            if not first:
                out = out + HB[k, rows, :]
            HB[k, rows, :] = out

    part_rows = lambda zz, yl: group_rows(2, zz * 64 + yl * 32, 32)
    fwd = []
    up, down, far = {}, {}, {}

    def forward(k, zz, yl):
        block = X.at[k, part_rows(zz, yl)]
        fwd.append(remote(block, block, to_sib))

    def spread(k, n):
        yl = 1 - ylo if n == 0 else ylo
        block = X.at[k, part_rows(z, yl)]
        up[k, n] = remote(block, block, to_z[0])
        down[k, n] = remote(block, block, to_z[1])
        forward(k, z, yl)

    def pass_on(k, n):
        yl = 1 - ylo if n == 0 else ylo
        if k == 0:
            up[k, n].wait_recv()
            block = X.at[k, part_rows(z_down, yl)]
            far[k, n] = remote(block, block, to_z[0])
            forward(k, z_down, yl)
        else:
            down[k, n].wait_recv()
            block = X.at[k, part_rows(z_up, yl)]
            far[k, n] = remote(block, block, to_z[1])
            forward(k, z_up, yl)

    def rest(k, n):
        yl = 1 - ylo if n == 0 else ylo
        if k == 0:
            down[k, n].wait_recv()
            forward(k, z_up, yl)
        else:
            up[k, n].wait_recv()
            forward(k, z_down, yl)

    def last(k, n):
        yl = 1 - ylo if n == 0 else ylo
        far[k, n].wait_recv()
        forward(k, z_far, yl)

    tok_m = [None] * 2

    def from_partner(k):
        tok_n[k].wait_recv()
        block = X.at[k, part_rows(z, 1 - ylo)]
        tok_m[k] = remote(block, block, to_ym)
        spread(k, 0)

    got(quad[1])
    ring(1)
    from_partner(0)
    gram_of(0)
    relays = [relay_right(0)]
    from_partner(1)
    to_member(2)
    to_member(3)
    relays += [relay_left(1)]
    tok_m[0].wait_recv()
    spread(0, 1)
    pass_on(0, 0)
    tok_m[1].wait_recv()
    spread(1, 1)
    pass_on(1, 0)
    got(tok_c)
    gram_of(1)
    got(quad[2])
    ring(2)
    rest(0, 0)
    rest(1, 0)
    got(quad[3])
    ring(3)
    hidden(yhi, x, first=True)
    pass_on(0, 1)
    pass_on(1, 1)
    last(0, 0)
    last(1, 0)
    relays += [relay_right(2)]
    rest(0, 1)
    rest(1, 1)
    relays += [relay_left(3)]
    last(0, 1)
    last(1, 1)
    got([from_left[1], from_left[3], from_right[0], from_right[2]])
    hidden(yhi, left)
    hidden(yhi, right)
    got(fwd)
    gram_of(2)
    gram_of(3)
    hidden(1 - yhi, x, first=True)
    hidden(1 - yhi, left)
    hidden(1 - yhi, right)
    got(relays)
    hidden(yhi, across)
    hidden(1 - yhi, across)

    SQ[...] = jnp.zeros_like(SQ)

    @pl.loop(0, 4)
    def _(g):
        rows = pl.ds(pl.multiple_of(g * GROUP, GROUP), GROUP)

        @pl.loop(0, 4)
        def _(s):
            part = pl.ds(pl.multiple_of(g * GROUP + s * 64, 64), 64)
            act, der = gelu_pair(HB[0, part, :])
            S1[0, part, :] = (HB[1, part, :] * der).astype(BF)
            S1[1, part, :] = act.astype(BF)

        @pl.loop(0, 2)
        def _(k):
            s = S1[k, rows, :]
            gs = dot(GM[k, 0, rows, :], s, ((1,), (0,))) + dot(GM[k, 1, rows, :], s, ((1,), (0,)))
            GS[k, rows, :] = gs
            row = jnp.sum(gs * s.astype(F32), axis=0, keepdims=True)
            row = row[:, :128] + row[:, 128:256] + row[:, 256:]
            SQ[pl.ds(g, 1), :] += row

    def exchange(slot, targets):
        sums = [remote(SQ, SQR.at[slot + i], t, keep=False) for i, t in enumerate(targets)]
        for copy in sums:
            copy.wait_recv()
            copy.wait_send()
        total = SQ[...]
        for i in range(len(targets)):
            total += SQR[slot + i]
        SQ[...] = total

    exchange(0, [to_sib])
    exchange(1, to_y)
    exchange(4, to_z)
    square = jnp.sum(SQ[...], axis=1, keepdims=True)
    FAC[...] = jnp.broadcast_to(RADIUS_SHARE * math.sqrt(D + FF) / jnp.sqrt(square + EPSILON), FAC.shape)

    @pl.loop(0, 16)
    def _(s):
        part = pl.ds(pl.multiple_of(s * 64, 64), 64)
        f = FAC[pl.ds(s // 4, 1), :][:, :1]
        act, der = gelu_pair(HB[0, part, :] + f * GS[0, part, :])
        S2[0, part, :] = ((HB[1, part, :] + f * GS[1, part, :]) * der).astype(BF)
        S2[1, part, :] = act.astype(BF)

    def term(xx, dy):
        yy = yhi if dy == 0 else 1 - yhi
        base = pl.ds(pl.multiple_of((yy * 4 + xx) * QUARTER, 128), QUARTER)

        @pl.loop(0, 2)
        def _(k):
            T[k, base, :] = dot(X[k, :, base], S2[k], ((0,), (0,))).astype(BF)

    def send_term(src_x, j, dst, target):
        return remote(T.at[:, rows_of(src_x, j)], dst, target)

    def input_rows(yy, cc, dst, add):
        g = yy * 2 + cc
        rows = pl.ds(pl.multiple_of(g * GROUP, GROUP), GROUP)
        f = FAC[pl.ds(g, 1), :][:, :1]
        cross = (f * dot(S2[0, rows, :], S1[0, rows, :], ((1,), (1,)))).astype(BF)

        @pl.loop(0, 4)
        def _(n):
            cols = pl.ds(pl.multiple_of(n * 768, 768), 768)
            out = dot(S2[0, rows, :], W[0, cols, :], ((1,), (1,))) + dot(cross, X[0, rows, cols], ((1,), (0,)))
            out = out.reshape(4, 2, 32, 768)
            if add is not None:
                out = out + add[yy, :, :, :, cols].astype(F32)
            dst[yy, :, :, :, cols] = out.astype(BF)

    hop = [None] * 4
    to_core = [None] * 2

    def first_rows(yy):
        input_rows(yy, 1 - c, PS, None)
        to_core[yy] = remote(PS.at[yy], PR.at[yy], to_sib)

    final_left, final_right = [None] * 4, [None] * 4
    first_rows(0)
    term(across, 1)
    hop[2] = send_term(across, 2, HOP.at[2], to_right)
    hop[3] = send_term(across, 3, HOP.at[3], to_left)
    first_rows(1)
    term(right, 1)
    final_left[3] = send_term(right, 3, FL.at[3], to_right)
    term(left, 1)
    final_right[2] = send_term(left, 2, FR.at[2], to_left)
    for yy in (0, 1):
        to_core[yy].wait_recv()
        input_rows(yy, c, PO, PR)
    halves, tail = (pl.ds(0, 1024), pl.ds(1024, 1024)), pl.ds(2048, 1024)
    z_hop = [
        remote(PO.at[:, z_far, :, :, halves[0]], ZH.at[0], to_z[0]),
        remote(PO.at[:, z_far, :, :, halves[1]], ZH.at[1], to_z[1]),
    ]
    yb = [remote(PO.at[y_of[i][0], :, y_of[i][1], :, tail], YB.at[i], to_y[i]) for i in range(3)]
    z_own = [
        remote(PO.at[:, z_down, :, :, halves[0]], ZF.at[0, 0], to_z[1]),
        remote(PO.at[:, z_up, :, :, halves[1]], ZF.at[1, 0], to_z[0]),
    ]

    def add_hop(xx, j):
        hop[j].wait_recv()
        rows = rows_of(xx, j)
        T[:, rows, :] = (T[:, rows, :].astype(F32) + HOP[j].astype(F32)).astype(BF)

    add_hop(right, 2)
    final_left[2] = send_term(right, 2, FL.at[2], to_right)
    add_hop(left, 3)
    final_right[3] = send_term(left, 3, FR.at[3], to_left)
    term(across, 0)
    hop[0] = send_term(across, 0, HOP.at[0], to_right)
    hop[1] = send_term(across, 1, HOP.at[1], to_left)
    z_sum = []
    for h, (zz, target) in enumerate(((z_up, to_z[0]), (z_down, to_z[1]))):
        z_hop[h].wait_recv()

        @pl.loop(0, 4)
        def _(i):
            a, b = i // 2, lax.rem(i, 2)
            block = PO[a, zz, b, :, halves[h]].astype(F32) + ZH[h, a, b].astype(F32)
            PO[a, zz, b, :, halves[h]] = block.astype(BF)

        z_sum.append(remote(PO.at[:, zz, :, :, halves[h]], ZF.at[h, 1], target))

    term(right, 0)
    final_left[1] = send_term(right, 1, FL.at[1], to_right)
    term(left, 0)
    final_right[0] = send_term(left, 0, FR.at[0], to_left)
    add_hop(right, 0)
    final_left[0] = send_term(right, 0, FL.at[0], to_right)
    add_hop(left, 1)
    final_right[1] = send_term(left, 1, FR.at[1], to_left)
    term(x, 1)
    term(x, 0)

    def total(j):
        final_left[j].wait_recv()
        final_right[j].wait_recv()
        OS[j] = (T[:, rows_of(x, j), :].astype(F32) + FL[j].astype(F32) + FR[j].astype(F32)).astype(BF)

    outs = []

    def deliver(j):
        total(j)
        mine = quarter_of(0)
        for k, out in enumerate((gin_out, gout_out)):
            if j == 0:
                own = pltpu.make_async_copy(OS.at[0, k], out.at[:, mine], local.at[k])
                own.start()
                kept.append(own)
            else:
                outs.append(remote(OS.at[j, k], out.at[:, mine], to_quad[j]))

    kept = []
    got(yb)

    @pl.loop(0, 4)
    def _(i):
        s = PO[yhi, i, ylo, :, tail].astype(F32)
        for slot in range(3):
            s += YB[slot, i].astype(F32)
        RB[i] = s.astype(BF)

    zb = [remote(RB.at[z_of[i]], ZB.at[i], to_z[i]) for i in range(3)]
    got(z_own)
    got(z_sum)

    @pl.loop(0, 4)
    def _(i):
        a, b = i // 2, lax.rem(i, 2)
        for h in (0, 1):
            s = PO[a, z, b, :, halves[h]].astype(F32)
            s += ZF[h, 0, a, b].astype(F32) + ZF[h, 1, a, b].astype(F32)
            RA[a, b, :, halves[h]] = s.astype(BF)

    ya = [remote(RA.at[y_of[i][0], y_of[i][1]], YA.at[i], to_y[i]) for i in range(3)]
    got(zb)
    s = RB[z].astype(F32)
    for slot in range(3):
        s += ZB[slot].astype(F32)
    IG[z, ylo, :, tail] = s.astype(BF)
    got(ya)
    s = RA[yhi, ylo].astype(F32)
    for slot in range(3):
        s += YA[slot].astype(F32)
    IG[z, ylo, :, pl.ds(0, 2048)] = s.astype(BF)

    ig_up, ig_down, ig_far = [None] * 2, [None] * 2, []

    def ig_spread(n):
        mine = IG.at[z, ylo if n == 0 else 1 - ylo]
        ig_up[n] = remote(mine, mine, to_z[0])
        ig_down[n] = remote(mine, mine, to_z[1])

    def ig_pass_on(n):
        yl = ylo if n == 0 else 1 - ylo
        ig_up[n].wait_recv()
        block = IG.at[z_down, yl, :, pl.ds(0, HALF)]
        ig_far.append(remote(block, block, to_z[0]))
        ig_down[n].wait_recv()
        block = IG.at[z_up, yl, :, pl.ds(HALF, HALF)]
        ig_far.append(remote(block, block, to_z[1]))

    ig_ym = remote(IG.at[z, ylo], IG.at[z, ylo], to_ym)
    ig_spread(0)
    deliver(2)
    deliver(3)
    ig_ym.wait_recv()
    ig_spread(1)
    deliver(1)
    deliver(0)
    ig_pass_on(0)
    ig_pass_on(1)
    got(ig_far)
    done = pltpu.make_async_copy(IG, input_out, local.at[2])
    done.start()
    got(outs)
    for own in kept:
        own.wait()
    done.wait()
    for copy in pending:
        copy.wait_send()


def on_device(tokens, cotangent, w_in, w_out):
    grad_scale = 1.0 / math.sqrt(TOKENS)
    any_space = pl.BlockSpec(memory_space=pl.ANY)
    vmem = pltpu.VMEM
    grad_in, grad_out, input_grad = pl.pallas_call(
        kernel,
        out_shape=(
            jax.ShapeDtypeStruct((ROWS, 4 * QUARTER), BF),
            jax.ShapeDtypeStruct((ROWS, 4 * QUARTER), BF),
            jax.ShapeDtypeStruct((4, 2, 32, D), BF),
        ),
        in_specs=[any_space] * 4,
        out_specs=(any_space,) * 3,
        scratch_shapes=[
            vmem((2, 4 * GROUP, D), BF),
            vmem((2, D, QUARTER), BF),
            vmem((2, 4 * GROUP, QUARTER), F32),
            vmem((2, 4 * GROUP, QUARTER), F32),
            vmem((2, 2, 4 * GROUP, GROUP), BF),
            vmem((2, 4 * GROUP, QUARTER), BF),
            vmem((2, 4 * GROUP, QUARTER), BF),
            vmem((2, D, QUARTER), BF),
            vmem((4, 2, ROWS, QUARTER), BF),
            vmem((4, 2, ROWS, QUARTER), BF),
            vmem((4, 2, ROWS, QUARTER), BF),
            vmem((4, 2, ROWS, QUARTER), BF),
            vmem((2, 4, 2, 32, D), BF),
            vmem((2, 4, 2, 32, D), BF),
            vmem((2, 4, 2, 32, D), BF),
            vmem((2, 2, 2, 32, 1024), BF),
            vmem((2, 2, 2, 2, 32, 1024), BF),
            vmem((3, 4, 32, 1024), BF),
            vmem((2, 2, 32, 2048), BF),
            vmem((4, 32, 1024), BF),
            vmem((3, 32, 2048), BF),
            vmem((3, 32, 1024), BF),
            vmem((4, 2, 32, D), BF),
            vmem((8, 128), F32),
            vmem((7, 8, 128), F32),
            vmem((8, 128), F32),
            pltpu.SemaphoreType.DMA((128,)),
            pltpu.SemaphoreType.DMA((128,)),
            pltpu.SemaphoreType.DMA((4,)),
        ],
        compiler_params=pltpu.CompilerParams(
            collective_id=0, has_side_effects=True, vmem_limit_bytes=63 * 2**20
        ),
        cost_estimate=pl.CostEstimate(flops=20 * 10**9, bytes_accessed=40 * 2**20, transcendentals=10**6),
    )(tokens, cotangent, w_in, w_out.T)
    return (
        grad_in.astype(F32) * grad_scale,
        (grad_out.astype(F32) * grad_scale).T,
        input_grad.reshape(GROUP, D),
    )


def solution(mesh):
    return jax.shard_map(
        on_device,
        mesh=mesh,
        in_specs=(P("fsdp", None), P("fsdp", None), P("fsdp", "dp"), P("dp", "fsdp")),
        out_specs=(P("fsdp", "dp"), P("dp", "fsdp"), P("fsdp", None)),
        check_vma=False,
    )
```

time: 158 us -> 138 us (0.87)
  Pallas kernels: 147 us -> 133 us
  local copies, waits for them, and re-layouts: 5.74 us -> 1.15 us
    pallas_call x1, Pallas kernels: 147 us -> 133 us  [on_device(): pl.pallas_call(kernel, out_shape=(jax.ShapeDtypeStruct((ROWS, 4 * QUARTER...]
    transpose x0 -> x1, other arithmetic: none -> 3.06 us  [on_device(): return (grad_in.astype(F32) * grad_scale, (grad_out.astype(F32) * grad_sc...]
    unnamed x5 -> x3, local copies, waits for them, and re-layouts: 4.06 us -> 1.15 us
    another operation x1 -> x0, other arithmetic: 2.36 us -> none  [on_device(): both = jnp.stack([w_in, w_out.T])]
    slice x3 -> x0, local copies, waits for them, and re-layouts: 1.68 us -> none  [on_device(): return (grads[0], grads[1].T, input_grad.reshape(GROUP, D))]
where the time goes in v3:
time: 138 us
  Pallas kernels  133 us (96%)
  other arithmetic  3.06 us (2%)
    pallas_call x1, Pallas kernels, on_device(): pl.pallas_call(kernel, out_shape=(jax.ShapeDtypeStruct((ROWS, 4 * QUARTER...  133 us
    transpose x1, other arithmetic, on_device(): return (grad_in.astype(F32) * grad_scale, (grad_out.astype(F32) * grad_sc...  3.06 us

profile of v3, /device:TPU:0, one launch (start us, length us, event | category | flops | bytes accessed | tf_op | source)
XLA Modules:
  0.0 137.9 jit_solution(13298943323438979444)
XLA Ops:
  0.6 133.0 %shard_map.67 = (bf16[192,1536]{1,0:T(8,128)(2,1)}, bf16[192,1536]{1,0:T(8,128)(2,1)}, bf16[4,2,32,3072]{3,2,1,0:T(8,128)(2,1)}) custom-call(bf16[256,3072]{1,0:T(8,128)(2,1)} %tok_ref.1, bf16[256,3072]{1,0:T(8,128)(2,1)} %cot_ref.1, bf16[192,1536]{1,0:T(8,128)(2,1)} %win_ref.1, bf16[192,1536]{1,0:T(8,128)(2,1)} %bitcast.5), custom_call_target="tpu_custom_call" | custom-call | flops 20000000000 | bytes 41943040 | tf_op jit(solution)/shard_map/pallas_call | solution.py:493
  133.7 0.0 copy-start
  133.7 3.1 %multiply_bitcast_fusion = (f32[1536,192]{0,1:T(8,128)}, f32[192,1536]{1,0:T(8,128)}) fusion(bf16[192,1536]{1,0:T(8,128)(2,1)} %get-tuple-element.7, bf16[192,1536]{1,0:T(8,128)(2,1)} %get-tuple-element.6), kind=kLoop, calls=%fused_computation | loop fusion | flops 1179648 | bytes 3538944 | tf_op jit(solution)/shard_map/transpose | solution.py:540
  136.7 0.0 copy-done
  136.7 1.1 copy.8
Async XLA Ops:
  133.7 3.1 %copy-start = (bf16[4,2,32,3072]{3,2,1,0:T(8,128)(2,1)S(1)}, bf16[4,2,32,3072]{3,2,1,0:T(8,128)(2,1)}, u32[]{:S(2)}) copy-start(bf16[4,2,32,3072]{3,2,1,0:T(8,128)(2,1)} %get-tuple-element.8) | copy-start | bytes 4718596

commit v4 on v3

--- a/solution.py
+++ b/solution.py
@@ -13,7 +13,7 @@
 GROUP = 256
 ROWS = 192
 QUARTER = 384
-HALF = 1536
+CHUNK = 768
 
 RADIUS_SHARE = 0.5
 EPSILON = 1e-06
@@ -34,7 +34,7 @@
 
 def kernel(
     tok_ref, cot_ref, win_ref, wout_ref, gin_out, gout_out, input_out,
-    X, W, HB, GS, GM, S1, S2, T, HOP, FL, FR, OS, PO, PS, PR, ZH, ZF, YB, RA, RB, YA, ZB, IG,
+    X, W, HB, GS, GM, S1, S2, T, HOP, FL, FR, OS, CR, PB, PR, ZH, ZF, RA, YA, IG, ST, SB,
     SQ, SQR, FAC, send, recv, local,
 ):
     dp, fs = lax.axis_index("dp"), lax.axis_index("fsdp")
@@ -51,6 +51,7 @@
     to_right, to_left = dev(z, ylo, yhi, right, c), dev(z, ylo, yhi, left, c)
     to_z = [dev(zz, ylo, yhi, x, c) for zz in (z_up, z_down, z_far)]
     to_yn, to_ym, to_y2 = dev(z, 1 - ylo, 1 - yhi, x, c), dev(z, 1 - ylo, yhi, x, c), to_quad[2]
+    to_ynx, to_ymx = dev(z, 1 - ylo, 1 - yhi, x, 1 - c), dev(z, 1 - ylo, yhi, x, 1 - c)
     to_y = [to_ym, to_yn, to_y2]
     y_of = [(yhi, 1 - ylo), (1 - yhi, 1 - ylo), (1 - yhi, ylo)]
     z_of = [z_up, z_down, z_far]
@@ -85,7 +86,7 @@
         return pl.ds(pl.multiple_of((yy * 2 + cc) * GROUP + start, 32), size)
 
     barrier = pltpu.get_barrier_semaphore()
-    peers = [to_sib, to_quad[2], to_quad[3], to_right, to_left, *to_z, to_yn, to_ym]
+    peers = [to_sib, to_quad[2], to_quad[3], to_right, to_left, *to_z, to_yn, to_ym, to_ynx, to_ymx]
     tokens_of, weights_of = (tok_ref, cot_ref), (win_ref, wout_ref)
     copies = [
         pltpu.make_async_copy(weights_of[k].at[:, quarter_of(0)], W.at[k, rows_of(x, 0)], local.at[k])
@@ -109,7 +110,16 @@
         return remote(tokens_of[k].at[rows], X.at[k, group_rows(0, z * 64 + ylo * 32, 32)], to_yn)
 
     tok_n = [to_partner(k) for k in (0, 1)]
+    stage = {
+        j: [remote(weights_of[k].at[:, quarter_of(j)], ST.at[j - 2, k], to_ym) for k in (0, 1)] for j in (2, 3)
+    }
     to_member(1)
+
+    def stage_on(j):
+        for copy in stage[j]:
+            copy.wait_recv()
+        quad[j] = [remote(ST.at[j - 2], W.at[:, rows_of(x, 0)], to_yn if j == 2 else to_ynx)]
+
     from_left, from_right = [None] * 4, [None] * 4
 
     def ring(j):
@@ -148,16 +158,13 @@
             GM[k, 0, rows, :] = hi
             GM[k, 1, rows, :] = (g - hi.astype(F32)).astype(BF)
 
-    def hidden(yy, xx, first=False):
-        @pl.loop(0, 4)
-        def _(i):
-            k = i // 2
-            rows = pl.ds(pl.multiple_of((yy * 2 + lax.rem(i, 2)) * GROUP, GROUP), GROUP)
-            out = None
-            for half in (0, 1):
-                base = pl.ds(pl.multiple_of((half * 4 + xx) * QUARTER, 128), QUARTER)
-                part = dot(X[k, rows, base], W[k, base, :], ((1,), (0,)))
-                out = part if out is None else out + part
+    def hidden(yy, xx, half, first=False):
+        base = pl.ds(pl.multiple_of((half * 4 + xx) * QUARTER, 128), QUARTER)
+        rows = pl.ds(pl.multiple_of(yy * 2 * GROUP, 2 * GROUP), 2 * GROUP)
+
+        @pl.loop(0, 2)
+        def _(k):
+            out = dot(X[k, rows, base], W[k, base, :], ((1,), (0,)))
             if not first:
                 out = out + HB[k, rows, :]
             HB[k, rows, :] = out
@@ -212,52 +219,62 @@
         tok_m[k] = remote(block, block, to_ym)
         spread(k, 0)
 
+    other = 1 - yhi
     got(quad[1])
     ring(1)
     from_partner(0)
     gram_of(0)
     relays = [relay_right(0)]
+    stage_on(2)
     from_partner(1)
-    to_member(2)
-    to_member(3)
+    pass_on(0, 0)
     relays += [relay_left(1)]
-    tok_m[0].wait_recv()
-    spread(0, 1)
-    pass_on(0, 0)
-    tok_m[1].wait_recv()
-    spread(1, 1)
+    stage_on(3)
+    rest(0, 0)
     pass_on(1, 0)
     got(tok_c)
     gram_of(1)
     got(quad[2])
     ring(2)
-    rest(0, 0)
+    tok_m[0].wait_recv()
+    spread(0, 1)
     rest(1, 0)
+    hidden(yhi, x, yhi, first=True)
+    tok_m[1].wait_recv()
+    spread(1, 1)
+    last(0, 0)
+    last(1, 0)
     got(quad[3])
     ring(3)
-    hidden(yhi, x, first=True)
+    got([from_left[1], from_right[0]])
+    hidden(yhi, left, yhi)
     pass_on(0, 1)
+    hidden(yhi, right, yhi)
+    got(relays)
+    hidden(yhi, across, yhi)
     pass_on(1, 1)
-    last(0, 0)
-    last(1, 0)
-    relays += [relay_right(2)]
     rest(0, 1)
     rest(1, 1)
-    relays += [relay_left(3)]
+    hidden(yhi, x, other)
+    late = [relay_right(2), relay_left(3)]
     last(0, 1)
     last(1, 1)
-    got([from_left[1], from_left[3], from_right[0], from_right[2]])
-    hidden(yhi, left)
-    hidden(yhi, right)
+    got([from_left[3], from_right[2]])
+    hidden(yhi, left, other)
+    hidden(yhi, right, other)
     got(fwd)
     gram_of(2)
     gram_of(3)
-    hidden(1 - yhi, x, first=True)
-    hidden(1 - yhi, left)
-    hidden(1 - yhi, right)
-    got(relays)
-    hidden(yhi, across)
-    hidden(1 - yhi, across)
+    hidden(other, x, yhi, first=True)
+    hidden(other, left, yhi)
+    hidden(other, right, yhi)
+    hidden(other, across, yhi)
+    hidden(other, x, other)
+    hidden(other, left, other)
+    hidden(other, right, other)
+    got(late)
+    hidden(yhi, across, other)
+    hidden(other, across, other)
 
     SQ[...] = jnp.zeros_like(SQ)
 
@@ -316,165 +333,195 @@
     def send_term(src_x, j, dst, target):
         return remote(T.at[:, rows_of(src_x, j)], dst, target)
 
-    def input_rows(yy, cc, dst, add):
-        g = yy * 2 + cc
-        rows = pl.ds(pl.multiple_of(g * GROUP, GROUP), GROUP)
-        f = FAC[pl.ds(g, 1), :][:, :1]
-        cross = (f * dot(S2[0, rows, :], S1[0, rows, :], ((1,), (1,)))).astype(BF)
-
-        @pl.loop(0, 4)
-        def _(n):
-            cols = pl.ds(pl.multiple_of(n * 768, 768), 768)
-            out = dot(S2[0, rows, :], W[0, cols, :], ((1,), (1,))) + dot(cross, X[0, rows, cols], ((1,), (0,)))
-            out = out.reshape(4, 2, 32, 768)
-            if add is not None:
-                out = out + add[yy, :, :, :, cols].astype(F32)
-            dst[yy, :, :, :, cols] = out.astype(BF)
-
-    hop = [None] * 4
-    to_core = [None] * 2
-
-    def first_rows(yy):
-        input_rows(yy, 1 - c, PS, None)
-        to_core[yy] = remote(PS.at[yy], PR.at[yy], to_sib)
-
-    final_left, final_right = [None] * 4, [None] * 4
-    first_rows(0)
-    term(across, 1)
-    hop[2] = send_term(across, 2, HOP.at[2], to_right)
-    hop[3] = send_term(across, 3, HOP.at[3], to_left)
-    first_rows(1)
-    term(right, 1)
-    final_left[3] = send_term(right, 3, FL.at[3], to_right)
-    term(left, 1)
-    final_right[2] = send_term(left, 2, FR.at[2], to_left)
-    for yy in (0, 1):
-        to_core[yy].wait_recv()
-        input_rows(yy, c, PO, PR)
-    halves, tail = (pl.ds(0, 1024), pl.ds(1024, 1024)), pl.ds(2048, 1024)
-    z_hop = [
-        remote(PO.at[:, z_far, :, :, halves[0]], ZH.at[0], to_z[0]),
-        remote(PO.at[:, z_far, :, :, halves[1]], ZH.at[1], to_z[1]),
-    ]
-    yb = [remote(PO.at[y_of[i][0], :, y_of[i][1], :, tail], YB.at[i], to_y[i]) for i in range(3)]
-    z_own = [
-        remote(PO.at[:, z_down, :, :, halves[0]], ZF.at[0, 0], to_z[1]),
-        remote(PO.at[:, z_up, :, :, halves[1]], ZF.at[1, 0], to_z[0]),
-    ]
+    hop, final_left, final_right = [None] * 4, [None] * 4, [None] * 4
 
     def add_hop(xx, j):
         hop[j].wait_recv()
         rows = rows_of(xx, j)
         T[:, rows, :] = (T[:, rows, :].astype(F32) + HOP[j].astype(F32)).astype(BF)
 
-    add_hop(right, 2)
-    final_left[2] = send_term(right, 2, FL.at[2], to_right)
-    add_hop(left, 3)
-    final_right[3] = send_term(left, 3, FR.at[3], to_left)
-    term(across, 0)
-    hop[0] = send_term(across, 0, HOP.at[0], to_right)
-    hop[1] = send_term(across, 1, HOP.at[1], to_left)
-    z_sum = []
-    for h, (zz, target) in enumerate(((z_up, to_z[0]), (z_down, to_z[1]))):
-        z_hop[h].wait_recv()
-
-        @pl.loop(0, 4)
-        def _(i):
-            a, b = i // 2, lax.rem(i, 2)
-            block = PO[a, zz, b, :, halves[h]].astype(F32) + ZH[h, a, b].astype(F32)
-            PO[a, zz, b, :, halves[h]] = block.astype(BF)
-
-        z_sum.append(remote(PO.at[:, zz, :, :, halves[h]], ZF.at[h, 1], target))
-
-    term(right, 0)
-    final_left[1] = send_term(right, 1, FL.at[1], to_right)
-    term(left, 0)
-    final_right[0] = send_term(left, 0, FR.at[0], to_left)
-    add_hop(right, 0)
-    final_left[0] = send_term(right, 0, FL.at[0], to_right)
-    add_hop(left, 1)
-    final_right[1] = send_term(left, 1, FR.at[1], to_left)
-    term(x, 1)
-    term(x, 0)
+    def first_hops(j):
+        term(across, j // 2)
+        hop[j] = send_term(across, j, HOP.at[j], to_right)
+        hop[j + 1] = send_term(across, j + 1, HOP.at[j + 1], to_left)
+
+    def directs(j):
+        term(right, j // 2)
+        final_left[j + 1] = send_term(right, j + 1, FL.at[j + 1], to_right)
+        term(left, j // 2)
+        final_right[j] = send_term(left, j, FR.at[j], to_left)
+
+    def sums(j):
+        add_hop(right, j)
+        final_left[j] = send_term(right, j, FL.at[j], to_right)
+        add_hop(left, j + 1)
+        final_right[j + 1] = send_term(left, j + 1, FR.at[j + 1], to_left)
 
     def total(j):
         final_left[j].wait_recv()
         final_right[j].wait_recv()
         OS[j] = (T[:, rows_of(x, j), :].astype(F32) + FL[j].astype(F32) + FR[j].astype(F32)).astype(BF)
 
-    outs = []
+    outs, kept, staged = [], [], {}
+    grad_outs = (gin_out, gout_out)
 
     def deliver(j):
         total(j)
-        mine = quarter_of(0)
-        for k, out in enumerate((gin_out, gout_out)):
+        if j >= 2:
+            staged[j] = remote(OS.at[j], SB.at[j - 2], to_yn)
+            return
+        for k in (0, 1):
+            place = grad_outs[k].at[:, quarter_of(0)]
             if j == 0:
-                own = pltpu.make_async_copy(OS.at[0, k], out.at[:, mine], local.at[k])
+                own = pltpu.make_async_copy(OS.at[0, k], place, local.at[k])
                 own.start()
                 kept.append(own)
             else:
-                outs.append(remote(OS.at[j, k], out.at[:, mine], to_quad[j]))
-
-    kept = []
-    got(yb)
+                outs.append(remote(OS.at[1, k], place, to_sib))
+
+    def deliver_on(j):
+        staged[j].wait_recv()
+        for k in (0, 1):
+            place = grad_outs[k].at[:, quarter_of(2)]
+            outs.append(remote(SB.at[j - 2, k], place, to_ym if j == 2 else to_ymx))
 
     @pl.loop(0, 4)
-    def _(i):
-        s = PO[yhi, i, ylo, :, tail].astype(F32)
+    def _(g):
+        rows = pl.ds(pl.multiple_of(g * GROUP, GROUP), GROUP)
+        f = FAC[pl.ds(g, 1), :][:, :1]
+        CR[rows, :] = (f * dot(S2[0, rows, :], S1[0, rows, :], ((1,), (1,)))).astype(BF)
+
+    to_core, z_hop, z_own, z_sum, y_part = {}, {}, {}, {}, {}
+
+    def cols_of(n):
+        return pl.ds(n * CHUNK, CHUNK)
+
+    def half_of(n, h):
+        return pl.ds(n * CHUNK + h * (CHUNK // 2), CHUNK // 2)
+
+    def partial(n):
+        cols = cols_of(n)
+
+        @pl.loop(0, 2)
+        def _(yy):
+            rows = pl.ds(pl.multiple_of(yy * 2 * GROUP, 2 * GROUP), 2 * GROUP)
+            out = dot(S2[0, rows, :], W[0, cols, :], ((1,), (1,)))
+            for cc in (0, 1):
+                group = pl.ds(pl.multiple_of((yy * 2 + cc) * GROUP, GROUP), GROUP)
+                mine = out[cc * GROUP : (cc + 1) * GROUP]
+                mine = mine + dot(CR[group, :], X[0, group, cols], ((1,), (0,)))
+                PB[yy, cc, :, :, :, cols] = mine.reshape(4, 2, 32, CHUNK).astype(BF)
+
+        to_core[n] = remote(PB.at[:, 1 - c, :, :, :, cols], PR.at[:, :, :, :, cols], to_sib)
+
+    def over_z(n):
+        cols = cols_of(n)
+        to_core[n].wait_recv()
+
+        @pl.loop(0, 8)
+        def _(i):
+            a, b = i // 4, lax.rem(i, 4)
+            both = PB[a, c, b, :, :, cols].astype(F32) + PR[a, b, :, :, cols].astype(F32)
+            PB[a, c, b, :, :, cols] = both.astype(BF)
+
+        part = lambda zz, h: PB.at[:, c, zz, :, :, half_of(n, h)]
+        z_hop[n] = [remote(part(z_far, h), ZH.at[n, h], to_z[h]) for h in (0, 1)]
+        z_own[n] = [remote(part(z_down, 0), ZF.at[n, 0, 0], to_z[1]), remote(part(z_up, 1), ZF.at[n, 1, 0], to_z[0])]
+
+    def z_relay(n):
+        z_sum[n] = []
+        for h, zz in enumerate((z_up, z_down)):
+            z_hop[n][h].wait_recv()
+            cols = half_of(n, h)
+            both = PB[:, c, zz, :, :, cols].astype(F32) + ZH[n, h].astype(F32)
+            PB[:, c, zz, :, :, cols] = both.astype(BF)
+            z_sum[n].append(remote(PB.at[:, c, zz, :, :, cols], ZF.at[n, h, 1], to_z[h]))
+
+    def over_y(n):
+        got(z_own[n])
+        got(z_sum[n])
+        for h in (0, 1):
+            cols = half_of(n, h)
+            s = PB[:, c, z, :, :, cols].astype(F32) + ZF[n, h, 0].astype(F32) + ZF[n, h, 1].astype(F32)
+            RA[:, :, :, cols] = s.astype(BF)
+        y_part[n] = [remote(RA.at[y_of[i][0], y_of[i][1], :, cols_of(n)], YA.at[n, i], to_y[i]) for i in range(3)]
+
+    ig_ym, ig_up, ig_down, ig_far = {}, {}, {}, []
+
+    def ig_send(n, m):
+        mine = IG.at[z, ylo if m == 0 else 1 - ylo, :, cols_of(n)]
+        ig_up[n, m] = remote(mine, mine, to_z[0])
+        ig_down[n, m] = remote(mine, mine, to_z[1])
+
+    def spread_rows(n):
+        got(y_part[n])
+        s = RA[yhi, ylo, :, cols_of(n)].astype(F32)
         for slot in range(3):
-            s += YB[slot, i].astype(F32)
-        RB[i] = s.astype(BF)
-
-    zb = [remote(RB.at[z_of[i]], ZB.at[i], to_z[i]) for i in range(3)]
-    got(z_own)
-    got(z_sum)
-
-    @pl.loop(0, 4)
-    def _(i):
-        a, b = i // 2, lax.rem(i, 2)
-        for h in (0, 1):
-            s = PO[a, z, b, :, halves[h]].astype(F32)
-            s += ZF[h, 0, a, b].astype(F32) + ZF[h, 1, a, b].astype(F32)
-            RA[a, b, :, halves[h]] = s.astype(BF)
-
-    ya = [remote(RA.at[y_of[i][0], y_of[i][1]], YA.at[i], to_y[i]) for i in range(3)]
-    got(zb)
-    s = RB[z].astype(F32)
-    for slot in range(3):
-        s += ZB[slot].astype(F32)
-    IG[z, ylo, :, tail] = s.astype(BF)
-    got(ya)
-    s = RA[yhi, ylo].astype(F32)
-    for slot in range(3):
-        s += YA[slot].astype(F32)
-    IG[z, ylo, :, pl.ds(0, 2048)] = s.astype(BF)
-
-    ig_up, ig_down, ig_far = [None] * 2, [None] * 2, []
-
-    def ig_spread(n):
-        mine = IG.at[z, ylo if n == 0 else 1 - ylo]
-        ig_up[n] = remote(mine, mine, to_z[0])
-        ig_down[n] = remote(mine, mine, to_z[1])
-
-    def ig_pass_on(n):
-        yl = ylo if n == 0 else 1 - ylo
-        ig_up[n].wait_recv()
-        block = IG.at[z_down, yl, :, pl.ds(0, HALF)]
+            s += YA[n, slot].astype(F32)
+        IG[z, ylo, :, cols_of(n)] = s.astype(BF)
+        mine = IG.at[z, ylo, :, cols_of(n)]
+        ig_ym[n] = remote(mine, mine, to_ym)
+        ig_send(n, 0)
+
+    def spread_other(n):
+        ig_ym[n].wait_recv()
+        ig_send(n, 1)
+
+    def spread_far(n, m):
+        yl = ylo if m == 0 else 1 - ylo
+        ig_up[n, m].wait_recv()
+        block = IG.at[z_down, yl, :, half_of(n, 0)]
         ig_far.append(remote(block, block, to_z[0]))
-        ig_down[n].wait_recv()
-        block = IG.at[z_up, yl, :, pl.ds(HALF, HALF)]
+        ig_down[n, m].wait_recv()
+        block = IG.at[z_up, yl, :, half_of(n, 1)]
         ig_far.append(remote(block, block, to_z[1]))
 
-    ig_ym = remote(IG.at[z, ylo], IG.at[z, ylo], to_ym)
-    ig_spread(0)
+    partial(0)
+    first_hops(2)
+    over_z(0)
+    partial(1)
+    directs(2)
+    over_z(1)
+    z_relay(0)
+    partial(2)
+    sums(2)
+    over_z(2)
+    first_hops(0)
+    z_relay(1)
+    over_y(0)
+    partial(3)
+    directs(0)
+    over_z(3)
+    z_relay(2)
+    over_y(1)
+    spread_rows(0)
+    term(x, 1)
     deliver(2)
+    z_relay(3)
+    over_y(2)
+    spread_other(0)
+    spread_rows(1)
     deliver(3)
-    ig_ym.wait_recv()
-    ig_spread(1)
+    sums(0)
+    spread_far(0, 0)
+    spread_far(0, 1)
+    over_y(3)
+    spread_other(1)
+    spread_rows(2)
+    deliver_on(2)
+    term(x, 0)
+    spread_far(1, 0)
+    spread_far(1, 1)
+    spread_other(2)
+    spread_rows(3)
+    deliver_on(3)
+    spread_far(2, 0)
+    spread_far(2, 1)
+    spread_other(3)
     deliver(1)
     deliver(0)
-    ig_pass_on(0)
-    ig_pass_on(1)
+    spread_far(3, 0)
+    spread_far(3, 1)
     got(ig_far)
     done = pltpu.make_async_copy(IG, input_out, local.at[2])
     done.start()
@@ -512,22 +559,21 @@
             vmem((4, 2, ROWS, QUARTER), BF),
             vmem((4, 2, ROWS, QUARTER), BF),
             vmem((4, 2, ROWS, QUARTER), BF),
+            vmem((4 * GROUP, GROUP), BF),
+            vmem((2, 2, 4, 2, 32, D), BF),
             vmem((2, 4, 2, 32, D), BF),
-            vmem((2, 4, 2, 32, D), BF),
-            vmem((2, 4, 2, 32, D), BF),
-            vmem((2, 2, 2, 32, 1024), BF),
-            vmem((2, 2, 2, 2, 32, 1024), BF),
-            vmem((3, 4, 32, 1024), BF),
-            vmem((2, 2, 32, 2048), BF),
-            vmem((4, 32, 1024), BF),
-            vmem((3, 32, 2048), BF),
-            vmem((3, 32, 1024), BF),
+            vmem((4, 2, 2, 2, 32, CHUNK // 2), BF),
+            vmem((4, 2, 2, 2, 2, 32, CHUNK // 2), BF),
+            vmem((2, 2, 32, D), BF),
+            vmem((4, 3, 32, CHUNK), BF),
             vmem((4, 2, 32, D), BF),
+            vmem((2, 2, ROWS, QUARTER), BF),
+            vmem((2, 2, ROWS, QUARTER), BF),
             vmem((8, 128), F32),
             vmem((7, 8, 128), F32),
             vmem((8, 128), F32),
-            pltpu.SemaphoreType.DMA((128,)),
-            pltpu.SemaphoreType.DMA((128,)),
+            pltpu.SemaphoreType.DMA((192,)),
+            pltpu.SemaphoreType.DMA((192,)),
             pltpu.SemaphoreType.DMA((4,)),
         ],
         compiler_params=pltpu.CompilerParams(

time: 138 us -> 131 us (0.949)
  Pallas kernels: 133 us -> 126 us
    pallas_call x1, Pallas kernels: 133 us -> 126 us  [on_device(): pl.pallas_call(kernel, out_shape=(jax.ShapeDtypeStruct((ROWS, 4 * QUARTER...]
where the time goes in v4:
time: 131 us; the launch traced here: 130 us
  Pallas kernels  126 us (96%)
  other arithmetic  3.06 us (2%)
    pallas_call x1, Pallas kernels, on_device(): pl.pallas_call(kernel, out_shape=(jax.ShapeDtypeStruct((ROWS, 4 * QUARTER...  126 us
    transpose x1, other arithmetic, on_device(): return (grad_in.astype(F32) * grad_scale, (grad_out.astype(F32) * grad_sc...  3.06 us

profile of v4, /device:TPU:0, one launch (start us, length us, event | category | flops | bytes accessed | tf_op | source)
XLA Modules:
  0.0 130.4 jit_solution(17412898117472152821)
XLA Ops:
  0.6 125.5 %shard_map.67 = (bf16[192,1536]{1,0:T(8,128)(2,1)}, bf16[192,1536]{1,0:T(8,128)(2,1)}, bf16[4,2,32,3072]{3,2,1,0:T(8,128)(2,1)}) custom-call(bf16[256,3072]{1,0:T(8,128)(2,1)} %tok_ref.1, bf16[256,3072]{1,0:T(8,128)(2,1)} %cot_ref.1, bf16[192,1536]{1,0:T(8,128)(2,1)} %win_ref.1, bf16[192,1536]{1,0:T(8,128)(2,1)} %bitcast.5), custom_call_target="tpu_custom_call" | custom-call | flops 20000000000 | bytes 41943040 | tf_op jit(solution)/shard_map/pallas_call | solution.py:540
  126.2 0.0 copy-start
  126.2 3.1 %multiply_bitcast_fusion = (f32[1536,192]{0,1:T(8,128)}, f32[192,1536]{1,0:T(8,128)}) fusion(bf16[192,1536]{1,0:T(8,128)(2,1)} %get-tuple-element.7, bf16[192,1536]{1,0:T(8,128)(2,1)} %get-tuple-element.6), kind=kLoop, calls=%fused_computation | loop fusion | flops 1179648 | bytes 3538944 | tf_op jit(solution)/shard_map/transpose | solution.py:586
  129.2 0.0 copy-done
  129.2 1.1 copy.8
Async XLA Ops:
  126.2 3.1 %copy-start = (bf16[4,2,32,3072]{3,2,1,0:T(8,128)(2,1)S(1)}, bf16[4,2,32,3072]{3,2,1,0:T(8,128)(2,1)}, u32[]{:S(2)}) copy-start(bf16[4,2,32,3072]{3,2,1,0:T(8,128)(2,1)} %get-tuple-element.8) | copy-start | bytes 4718596

commit v5 on v4

--- a/solution.py
+++ b/solution.py
@@ -158,13 +158,16 @@
             GM[k, 0, rows, :] = hi
             GM[k, 1, rows, :] = (g - hi.astype(F32)).astype(BF)
 
-    def hidden(yy, xx, half, first=False):
+    def hidden(yy, xx, half, first=False, both=False):
         base = pl.ds(pl.multiple_of((half * 4 + xx) * QUARTER, 128), QUARTER)
         rows = pl.ds(pl.multiple_of(yy * 2 * GROUP, 2 * GROUP), 2 * GROUP)
 
         @pl.loop(0, 2)
         def _(k):
             out = dot(X[k, rows, base], W[k, base, :], ((1,), (0,)))
+            if both:
+                rest = pl.ds(pl.multiple_of((4 + xx) * QUARTER, 128), QUARTER)
+                out = out + dot(X[k, rows, rest], W[k, rest, :], ((1,), (0,)))
             if not first:
                 out = out + HB[k, rows, :]
             HB[k, rows, :] = out
@@ -265,13 +268,10 @@
     got(fwd)
     gram_of(2)
     gram_of(3)
-    hidden(other, x, yhi, first=True)
-    hidden(other, left, yhi)
-    hidden(other, right, yhi)
+    hidden(other, x, 0, first=True, both=True)
+    hidden(other, left, 0, both=True)
+    hidden(other, right, 0, both=True)
     hidden(other, across, yhi)
-    hidden(other, x, other)
-    hidden(other, left, other)
-    hidden(other, right, other)
     got(late)
     hidden(yhi, across, other)
     hidden(other, across, other)
@@ -308,9 +308,8 @@
             total += SQR[slot + i]
         SQ[...] = total
 
-    exchange(0, [to_sib])
-    exchange(1, to_y)
-    exchange(4, to_z)
+    exchange(0, [to_sib, *to_y, to_quad[3], to_ynx, to_ymx])
+    exchange(7, to_z)
     square = jnp.sum(SQ[...], axis=1, keepdims=True)
     FAC[...] = jnp.broadcast_to(RADIUS_SHARE * math.sqrt(D + FF) / jnp.sqrt(square + EPSILON), FAC.shape)
 
@@ -498,11 +497,11 @@
     term(x, 1)
     deliver(2)
     z_relay(3)
+    sums(0)
     over_y(2)
     spread_other(0)
     spread_rows(1)
     deliver(3)
-    sums(0)
     spread_far(0, 0)
     spread_far(0, 1)
     over_y(3)
@@ -570,7 +569,7 @@
             vmem((2, 2, ROWS, QUARTER), BF),
             vmem((2, 2, ROWS, QUARTER), BF),
             vmem((8, 128), F32),
-            vmem((7, 8, 128), F32),
+            vmem((10, 8, 128), F32),
             vmem((8, 128), F32),
             pltpu.SemaphoreType.DMA((192,)),
             pltpu.SemaphoreType.DMA((192,)),

time: 131 us -> 129 us (0.985)
  Pallas kernels: 126 us -> 124 us
    pallas_call x1, Pallas kernels: 126 us -> 124 us  [on_device(): pl.pallas_call(kernel, out_shape=(jax.ShapeDtypeStruct((ROWS, 4 * QUARTER...]
where the time goes in v5:
time: 129 us
  Pallas kernels  124 us (96%)
  other arithmetic  3.06 us (2%)
    pallas_call x1, Pallas kernels, on_device(): pl.pallas_call(kernel, out_shape=(jax.ShapeDtypeStruct((ROWS, 4 * QUARTER...  124 us
    transpose x1, other arithmetic, on_device(): return (grad_in.astype(F32) * grad_scale, (grad_out.astype(F32) * grad_sc...  3.06 us

profile of v5, /device:TPU:0, one launch (start us, length us, event | category | flops | bytes accessed | tf_op | source)
XLA Modules:
  0.0 128.7 jit_solution(14133296581491895771)
XLA Ops:
  0.6 123.9 %shard_map.67 = (bf16[192,1536]{1,0:T(8,128)(2,1)}, bf16[192,1536]{1,0:T(8,128)(2,1)}, bf16[4,2,32,3072]{3,2,1,0:T(8,128)(2,1)}) custom-call(bf16[256,3072]{1,0:T(8,128)(2,1)} %tok_ref.1, bf16[256,3072]{1,0:T(8,128)(2,1)} %cot_ref.1, bf16[192,1536]{1,0:T(8,128)(2,1)} %win_ref.1, bf16[192,1536]{1,0:T(8,128)(2,1)} %bitcast.5), custom_call_target="tpu_custom_call" | custom-call | flops 20000000000 | bytes 41943040 | tf_op jit(solution)/shard_map/pallas_call | solution.py:539
  124.5 0.0 copy-start
  124.5 3.1 %multiply_bitcast_fusion = (f32[1536,192]{0,1:T(8,128)}, f32[192,1536]{1,0:T(8,128)}) fusion(bf16[192,1536]{1,0:T(8,128)(2,1)} %get-tuple-element.7, bf16[192,1536]{1,0:T(8,128)(2,1)} %get-tuple-element.6), kind=kLoop, calls=%fused_computation | loop fusion | flops 1179648 | bytes 3538944 | tf_op jit(solution)/shard_map/transpose | solution.py:585
  127.6 0.0 copy-done
  127.6 1.1 copy.8
Async XLA Ops:
  124.5 3.1 %copy-start = (bf16[4,2,32,3072]{3,2,1,0:T(8,128)(2,1)S(1)}, bf16[4,2,32,3072]{3,2,1,0:T(8,128)(2,1)}, u32[]{:S(2)}) copy-start(bf16[4,2,32,3072]{3,2,1,0:T(8,128)(2,1)} %get-tuple-element.8) | copy-start | bytes 4718596

commit v6 on v5

--- a/solution.py
+++ b/solution.py
@@ -13,7 +13,7 @@
 GROUP = 256
 ROWS = 192
 QUARTER = 384
-CHUNK = 768
+CHUNK = 1024
 
 RADIUS_SHARE = 0.5
 EPSILON = 1e-06
@@ -482,21 +482,18 @@
     directs(2)
     over_z(1)
     z_relay(0)
+    sums(2)
     partial(2)
-    sums(2)
     over_z(2)
     first_hops(0)
     z_relay(1)
     over_y(0)
-    partial(3)
     directs(0)
-    over_z(3)
     z_relay(2)
     over_y(1)
     spread_rows(0)
     term(x, 1)
     deliver(2)
-    z_relay(3)
     sums(0)
     over_y(2)
     spread_other(0)
@@ -504,23 +501,18 @@
     deliver(3)
     spread_far(0, 0)
     spread_far(0, 1)
-    over_y(3)
     spread_other(1)
     spread_rows(2)
     deliver_on(2)
     term(x, 0)
     spread_far(1, 0)
     spread_far(1, 1)
+    deliver_on(3)
     spread_other(2)
-    spread_rows(3)
-    deliver_on(3)
+    deliver(1)
+    deliver(0)
     spread_far(2, 0)
     spread_far(2, 1)
-    spread_other(3)
-    deliver(1)
-    deliver(0)
-    spread_far(3, 0)
-    spread_far(3, 1)
     got(ig_far)
     done = pltpu.make_async_copy(IG, input_out, local.at[2])
     done.start()
@@ -561,10 +553,10 @@
             vmem((4 * GROUP, GROUP), BF),
             vmem((2, 2, 4, 2, 32, D), BF),
             vmem((2, 4, 2, 32, D), BF),
-            vmem((4, 2, 2, 2, 32, CHUNK // 2), BF),
-            vmem((4, 2, 2, 2, 2, 32, CHUNK // 2), BF),
+            vmem((3, 2, 2, 2, 32, CHUNK // 2), BF),
+            vmem((3, 2, 2, 2, 2, 32, CHUNK // 2), BF),
             vmem((2, 2, 32, D), BF),
-            vmem((4, 3, 32, CHUNK), BF),
+            vmem((3, 3, 32, CHUNK), BF),
             vmem((4, 2, 32, D), BF),
             vmem((2, 2, ROWS, QUARTER), BF),
             vmem((2, 2, ROWS, QUARTER), BF),

time: 129 us -> 133 us (1.031); the launches traced: 129 us -> 131 us
  Pallas kernels: 124 us -> 126 us
    pallas_call x1, Pallas kernels: 124 us -> 126 us  [on_device(): pl.pallas_call(kernel, out_shape=(jax.ShapeDtypeStruct((ROWS, 4 * QUARTER...]
where the time goes in v6:
time: 133 us; the launch traced here: 131 us
  Pallas kernels  126 us (95%)
  other arithmetic  3.06 us (2%)
    pallas_call x1, Pallas kernels, on_device(): pl.pallas_call(kernel, out_shape=(jax.ShapeDtypeStruct((ROWS, 4 * QUARTER...  126 us
    transpose x1, other arithmetic, on_device(): return (grad_in.astype(F32) * grad_scale, (grad_out.astype(F32) * grad_sc...  3.06 us

profile of v6, /device:TPU:0, one launch (start us, length us, event | category | flops | bytes accessed | tf_op | source)
XLA Modules:
  0.0 131.3 jit_solution(12392734726880250165)
XLA Ops:
  0.6 126.5 %shard_map.67 = (bf16[192,1536]{1,0:T(8,128)(2,1)}, bf16[192,1536]{1,0:T(8,128)(2,1)}, bf16[4,2,32,3072]{3,2,1,0:T(8,128)(2,1)}) custom-call(bf16[256,3072]{1,0:T(8,128)(2,1)} %tok_ref.1, bf16[256,3072]{1,0:T(8,128)(2,1)} %cot_ref.1, bf16[192,1536]{1,0:T(8,128)(2,1)} %win_ref.1, bf16[192,1536]{1,0:T(8,128)(2,1)} %bitcast.5), custom_call_target="tpu_custom_call" | custom-call | flops 20000000000 | bytes 41943040 | tf_op jit(solution)/shard_map/pallas_call | solution.py:531
  127.1 0.0 copy-start
  127.1 3.1 %multiply_bitcast_fusion = (f32[1536,192]{0,1:T(8,128)}, f32[192,1536]{1,0:T(8,128)}) fusion(bf16[192,1536]{1,0:T(8,128)(2,1)} %get-tuple-element.7, bf16[192,1536]{1,0:T(8,128)(2,1)} %get-tuple-element.6), kind=kLoop, calls=%fused_computation | loop fusion | flops 1179648 | bytes 3538944 | tf_op jit(solution)/shard_map/transpose | solution.py:577
  130.2 0.0 copy-done
  130.2 1.1 copy.8
Async XLA Ops:
  127.1 3.1 %copy-start = (bf16[4,2,32,3072]{3,2,1,0:T(8,128)(2,1)S(1)}, bf16[4,2,32,3072]{3,2,1,0:T(8,128)(2,1)}, u32[]{:S(2)}) copy-start(bf16[4,2,32,3072]{3,2,1,0:T(8,128)(2,1)} %get-tuple-element.8) | copy-start | bytes 4718596
